TPU v7x, 32 devices: a whole 2x2x4 slice. The times are simulated.
32 devices in a mesh: tx: 4 (over y, x), ty: 8 (over z, core).
Axes of the slice: x: 2, y: 2, z: 4, core: 2. Of those that a mesh axis runs over, the one named last changes fastest.
Arguments:
- members: bfloat16 [32, 32, 512, 128], P('tx', 'ty'), may hold values from -4 to 4
- mean_state: float32 [32, 32, 512], P('tx', 'ty'), may hold values from -6 to 6
- obs_pert: bfloat16 [32, 32, 128, 128], P('tx', 'ty'), may hold values from -1.5 to 1.5
- obs_rinv: bfloat16 [32, 32, 128], P('tx', 'ty'), may hold values from 0.25 to 2
- innovation: bfloat16 [32, 32, 128], P('tx', 'ty'), may hold values from -12 to 12
- obs_count: int32 [32, 32], P('tx', 'ty'), may hold values from 1 to 128, as said below
- neighbours: int32 [32, 32, 12], P('tx', 'ty'), may hold values from 0 to 24, as said below
- loc_weight: float32 [32, 32, 12], P('tx', 'ty'), may hold values from 0.1 to 1
Outputs:
- analysis: bfloat16 [32, 32, 512, 128], P('tx', 'ty')
Inputs may be any that keep to these rules, and one draw needn't show every extreme that they name: `obs_count`: counts run from 1 to 128; 128 is reached on some blocks of every device. `neighbours`: the 12 codes of a group are distinct, each naming an offset (c // 5 - 2, c % 5 - 2) of at most two blocks per direction.
All inputs are finite; a program needn't handle non-finite values.
Results may differ from a plain program's by a relative error of at most 0.0049.
Values may be sent and summed in bfloat16 or wider, within the bound.
A program may use at most 128 MiB of HBM per device.

v0:
```python
import jax
import jax.numpy as jnp
from jax import lax
from jax.sharding import PartitionSpec as P

NSI = 5


def with_halo(block, sides, width):
    for axis, dim in sides:
        count = lax.axis_size(axis)
        forward = [(i, i + 1) for i in range(count - 1)]
        forward.append((count - 1, 0))
        backward = [(target, source) for source, target in forward]
        low = lax.ppermute(
            lax.slice_in_dim(block, block.shape[dim] - width, None, axis=dim), axis, forward
        )
        high = lax.ppermute(lax.slice_in_dim(block, 0, width, axis=dim), axis, backward)
        block = jnp.concatenate([low, block, high], axis=dim)
    return block


def transform(cmat, vsum, rho):
    width = cmat.shape[-1]
    identity = jnp.eye(width, dtype=jnp.float32)
    matrix = cmat + (width - 1) / rho * identity
    cnorm = jnp.sqrt(jnp.sum(matrix * matrix, axis=(1, 2)))[:, None, None]
    root_iter = matrix / cnorm
    inv_iter = jnp.broadcast_to(identity, matrix.shape)
    for sweep in range(NSI):
        update = 1.5 * identity - 0.5 * jnp.einsum(
            "gkl,glm->gkm", inv_iter, root_iter, precision=lax.Precision.HIGHEST
        )
        root_iter = jnp.einsum("gkl,glm->gkm", root_iter, update, precision=lax.Precision.HIGHEST)
        inv_iter = jnp.einsum("gkl,glm->gkm", update, inv_iter, precision=lax.Precision.HIGHEST)
    covar = jnp.einsum("gkl,glm->gkm", inv_iter, inv_iter, precision=lax.Precision.HIGHEST) / cnorm
    wbar = jnp.einsum("gkl,gl->gk", covar, vsum, precision=lax.Precision.HIGHEST)
    return jnp.sqrt(jnp.float32(width - 1)) * inv_iter / jnp.sqrt(cnorm) + wbar[:, :, None]


def block_terms(pert_blocks, packed):
    obs_weight = packed[:, :, 0, :].astype(jnp.float32)
    scaled = (pert_blocks.astype(jnp.float32) * obs_weight[..., None]).astype(jnp.bfloat16)
    grams = jnp.einsum("abok,abol->abkl", scaled, pert_blocks, preferred_element_type=jnp.float32)
    vectors = jnp.einsum(
        "abok,abo->abk", scaled, packed[:, :, 1, :], preferred_element_type=jnp.float32
    )
    return (grams, vectors)


def group_weights(grams, vectors, codes, listed_weight, rho):
    groups_x, groups_y, listed = codes.shape
    width = grams.shape[-1]
    outer_x = groups_x + 4
    outer_y = groups_y + 4
    row_pos = jnp.arange(groups_x, dtype=jnp.int32)[:, None, None]
    col_pos = jnp.arange(groups_y, dtype=jnp.int32)[None, :, None]
    target = (row_pos + codes // 5) * outer_y + (col_pos + codes % 5)
    hits = (target[..., None] == jnp.arange(outer_x * outer_y, dtype=jnp.int32)).astype(jnp.float32)
    picker = jnp.sum(listed_weight[..., None] * hits, axis=2).reshape(
        groups_x * groups_y, outer_x * outer_y
    )
    cmat = jnp.dot(
        picker, grams.reshape(outer_x * outer_y, width * width), precision=lax.Precision.HIGHEST
    )
    vsum = jnp.dot(
        picker, vectors.reshape(outer_x * outer_y, width), precision=lax.Precision.HIGHEST
    )
    weights = transform(cmat.reshape(groups_x * groups_y, width, width), vsum, rho)
    return weights.reshape(groups_x, groups_y, width, width)


def shards(members, mean_state, obs_pert, obs_rinv, innovation, obs_count, neighbours, loc_weight):
    blocks_x, blocks_y, slot_count, width = obs_pert.shape
    slots = jnp.arange(slot_count, dtype=jnp.int32)
    live_slot = slots[None, None, :] < obs_count[:, :, None]
    obs_weight = jnp.where(live_slot, obs_rinv.astype(jnp.float32), jnp.float32(0.0))
    innov_f = innovation.astype(jnp.float32)
    square_sum = jnp.sum(jnp.square(obs_pert.astype(jnp.float32)), axis=-1)
    first_sum, second_sum = lax.psum(
        (
            jnp.sum(obs_weight * innov_f * innov_f),
            jnp.sum(live_slot.astype(jnp.float32) + obs_weight * square_sum / (width - 1)),
        ),
        ("tx", "ty"),
    )
    rho = first_sum / second_sum
    packed = jnp.stack([obs_weight.astype(jnp.bfloat16), innovation], axis=2)
    outer_pert, outer_packed = (
        with_halo(obs_pert, (("tx", 0), ("ty", 1)), 2),
        with_halo(packed, (("tx", 0), ("ty", 1)), 2),
    )
    grams, vectors = block_terms(outer_pert, outer_packed)
    weights = group_weights(grams, vectors, neighbours, loc_weight, rho)
    framed = with_halo(weights, (("tx", 0), ("ty", 1)), 1)
    centre = framed[1:-1, 1:-1]
    blended = (
        4.0 * centre + framed[2:, 1:-1] + framed[:-2, 1:-1] + framed[1:-1, 2:] + framed[1:-1, :-2]
    ) / 8.0
    blended = blended.astype(jnp.bfloat16)
    result = jnp.einsum("abrk,abkm->abrm", members, blended, preferred_element_type=jnp.float32)
    return (result + mean_state[..., None]).astype(jnp.bfloat16)


def solution(mesh):
    return jax.shard_map(
        shards,
        mesh=mesh,
        in_specs=(
            P("tx", "ty", None, None),
            P("tx", "ty", None),
            P("tx", "ty", None, None),
            P("tx", "ty", None),
            P("tx", "ty", None),
            P("tx", "ty"),
            P("tx", "ty", None),
            P("tx", "ty", None),
        ),
        out_specs=P("tx", "ty", None, None),
        check_vma=False,
    )
```

profile of v0, /device:TPU:0, one launch (start us, length us, event | category | flops | bytes accessed | tf_op | source)
XLA Modules:
  0.0 188.6 jit_solution(4505629840472110320)
XLA Ops:
  4.9 3.0 %collective-permute-start.4 = (bf16[2,4,2,128]{3,1,0,2:T(4,128)(2,1)S(1)}, bf16[2,4,2,128]{3,1,0,2:T(4,128)(2,1)S(1)}, u32[]{:S(2)}, u32[]{:S(2)}) collective-permute-start(bf16[2,4,2,128]{3,1,0,2:T(4,128)(2,1)S(1)} %get-tuple-element.21), channel_id=1, source_target_pairs={{0,8},{8,16},{16,24},{24,0},{1,9},{9,17},{17,25},{25,1},{2,10},{10... | collective-permute-start | bytes 12296 | tf_op jit(solution)/shard_map/ppermute | solution.py:15
  12.5 45.6 %all-reduce = (f32[]{:T(128)}, f32[]{:T(128)}) all-reduce(f32[]{:T(128)} %get-tuple-element.6, f32[]{:T(128)} %get-tuple-element.5), channel_id=1, replica_groups=mesh['tx'=4,'ty'=8] {'tx','ty'}, use_global_device_ids=true, to_apply=%region_3.4 | all-reduce | flops 2 | bytes 16 | tf_op jit(solution)/shard_map/psum | solution.py:80
  59.9 3.5 %collective-permute-start.3 = (bf16[12,2,128,128]{3,2,1,0:T(8,128)(2,1)S(1)}, bf16[12,2,128,128]{3,2,1,0:T(8,128)(2,1)S(1)}, u32[]{:S(2)}, u32[]{:S(2)}) collective-permute-start(bf16[12,2,128,128]{3,2,1,0:T(8,128)(2,1)S(1)} %get-tuple-element.14), channel_id=1, source_target_pairs={{1,0},{2,1},{3,2},{4,3},{5,4},{6,5},{7,6},{0,7},{9,8},{10,9},{11,1... | collective-permute-start | bytes 2359304 | tf_op jit(solution)/shard_map/ppermute | solution.py:18
  63.6 3.5 %collective-permute-start.7 = (bf16[12,2,2,128]{3,1,0,2:T(2,128)(2,1)S(1)}, bf16[12,2,2,128]{3,1,0,2:T(2,128)(2,1)S(1)}, u32[]{:S(2)}, u32[]{:S(2)}) collective-permute-start(bf16[12,2,2,128]{3,1,0,2:T(2,128)(2,1)S(1)} %get-tuple-element.20), channel_id=1, source_target_pairs={{1,0},{2,1},{3,2},{4,3},{5,4},{6,5},{7,6},{0,7},{9,8},{10,9},{11,1... | collective-permute-start | bytes 36872 | tf_op jit(solution)/shard_map/ppermute | solution.py:18
  67.2 14.6 %collective-permute-done.6 = bf16[12,2,2,128]{3,1,0,2:T(2,128)(2,1)S(1)} collective-permute-done((bf16[12,2,2,128]{3,1,0,2:T(2,128)(2,1)S(1)}, bf16[12,2,2,128]{3,1,0,2:T(2,128)(2,1)S(1)}, u32[]{:S(2)}, u32[]{:S(2)}) %collective-permute-start.6) | collective-permute-done | bytes 12320 | tf_op jit(solution)/shard_map/ppermute | solution.py:15
  81.9 6.0 %fusion.8 = f32[12,8,128,128]{3,2,1,0:T(8,128)S(1)} fusion(f32[12,8,128]{2,1,0:T(8,128)S(1)} %get-tuple-element.18, bf16[12,2,128,128]{3,2,1,0:T(8,128)(2,1)S(1)} %collective-permute-done.3, bf16[12,4,128,128]{3,2,1,0:T(8,128)(2,1)S(1)} %constant_dynamic-update-slice_fusion, bf16[12,2,128,128]{3,2,1,0:T(8,128)(2,1)S(1)} %collective-permute-done.2), kind=kOutput, calls=%fused_computation.12 | convolution fusion | flops 413663232 | bytes 9486336 | tf_op jit(solution)/shard_map/abok,abol->abkl/dot_general | solution.py:44
  87.9 6.8 %multiply_reduce_fusion = (f32[32]{0:T(128)S(1)}, f32[32,128,128]{2,0,1:T(8,128)S(1)}) fusion(f32[128,128]{1,0:T(8,128)S(1)} %fusion.54, f32[32,96,1]{1,0,2:T(8,128)S(1)} %bitcast.70, f32[12,8,128,128]{3,2,1,0:T(8,128)S(1)} %fusion.8), kind=kOutput, calls=%fused_computation.38 | convolution fusion | flops 605552640 | bytes 8466560 | tf_op jit(solution)/shard_map/dot_general | solution.py:63
  95.3 3.2 %fusion.22 = f32[32,128,128]{2,1,0:T(8,128)S(1)} fusion(f32[32,128,128]{2,0,1:T(8,128)S(1)} %add_divide_fusion, f32[128,128]{1,0:T(8,128)S(1)} %fusion.55), kind=kOutput, calls=%fused_computation.42 | convolution fusion | flops 805306368 | bytes 4259840 | tf_op jit(solution)/shard_map/gkl,glm->gkm/dot_general | solution.py:31
  98.4 3.6 %fusion.20 = f32[32,128,128]{2,1,0:T(8,128)S(1)} fusion(f32[32,128,128]{2,0,1:T(8,128)S(1)} %add_divide_fusion, f32[32,128,128]{2,1,0:T(8,128)S(1)} %fusion.22, f32[128,128]{1,0:T(8,128)S(1)} %fusion.56), kind=kOutput, calls=%fused_computation.40 | convolution fusion | flops 806354944 | bytes 6356992 | tf_op jit(solution)/shard_map/gkl,glm->gkm/dot_general | solution.py:34
  108.6 2.4 %fusion.26 = f32[32,128,128]{2,1,0:T(8,128)S(1)} fusion(f32[32,128,128]{2,1,0:T(8,128)S(1)} %fusion.24, f32[32,128,128]{2,1,0:T(8,128)S(1)} %fusion.83, f32[128,128]{1,0:T(8,128)S(1)} %fusion.56), kind=kOutput, calls=%fused_computation.47 | convolution fusion | flops 806354944 | bytes 6356992 | tf_op jit(solution)/shard_map/gkl,glm->gkm/dot_general | solution.py:35
  111.0 2.5 %fusion.84 = f32[32,128,128]{2,1,0:T(8,128)S(1)} fusion(f32[32,128,128]{2,1,0:T(8,128)S(1)} %fusion.26, f32[32,128,128]{2,1,0:T(8,128)S(1)} %fusion.25), kind=kOutput, calls=%fused_computation.130 | convolution fusion | flops 805306368 | bytes 6291456 | tf_op jit(solution)/shard_map/gkl,glm->gkm/dot_general | solution.py:31
  115.8 2.4 %fusion.28 = f32[32,128,128]{2,1,0:T(8,128)S(1)} fusion(f32[32,128,128]{2,1,0:T(8,128)S(1)} %fusion.26, f32[32,128,128]{2,1,0:T(8,128)S(1)} %fusion.84, f32[128,128]{1,0:T(8,128)S(1)} %fusion.56), kind=kOutput, calls=%fused_computation.49 | convolution fusion | flops 806354944 | bytes 6356992 | tf_op jit(solution)/shard_map/gkl,glm->gkm/dot_general | solution.py:35
  120.5 2.4 %fusion.30 = f32[32,128,128]{2,1,0:T(8,128)S(1)} fusion(f32[32,128,128]{2,1,0:T(8,128)S(1)} %fusion.28, f32[32,128,128]{2,1,0:T(8,128)S(1)} %fusion.85, f32[128,128]{1,0:T(8,128)S(1)} %fusion.56), kind=kOutput, calls=%fused_computation.51 | convolution fusion | flops 806354944 | bytes 6356992 | tf_op jit(solution)/shard_map/gkl,glm->gkm/dot_general | solution.py:35
  122.9 2.7 %fusion.29 = f32[32,128,128]{2,1,0:T(8,128)S(1)} fusion(f32[32,128,128]{2,1,0:T(8,128)S(1)} %fusion.27, f32[32,128,128]{2,1,0:T(8,128)S(1)} %fusion.85, f32[128,128]{1,0:T(8,128)S(1)} %fusion.56), kind=kOutput, calls=%fused_computation.50 | convolution fusion | flops 806354944 | bytes 6356992 | tf_op jit(solution)/shard_map/gkl,glm->gkm/dot_general | solution.py:34
  127.9 2.4 %fusion.17 = f32[32,128,128]{2,1,0:T(8,128)S(1)} fusion(f32[32,128,128]{2,1,0:T(8,128)S(1)} %fusion.30, f32[32,128,128]{2,1,0:T(8,128)S(1)} %fusion.86, f32[128,128]{1,0:T(8,128)S(1)} %fusion.56), kind=kOutput, calls=%fused_computation.31 | convolution fusion | flops 806354944 | bytes 6356992 | tf_op jit(solution)/shard_map/gkl,glm->gkm/dot_general | solution.py:35
  133.7 2.9 %fusion.3 = f32[12,8,1,128]{3,2,1,0:T(1,128)S(1)} fusion(f32[12,8,128]{2,1,0:T(8,128)S(1)} %get-tuple-element.18, bf16[12,2,128,128]{3,2,1,0:T(8,128)(2,1)S(1)} %collective-permute-done.3, bf16[12,4,128,128]{3,2,1,0:T(8,128)(2,1)S(1)} %constant_dynamic-update-slice_fusion, bf16[12,2,128,128]{3,2,1,0:T(8,128)(2,1)S(1)} %collective-permute-done.2, ...), kind=kOutput, calls=%fused_computation.6 | convolution fusion | flops 11010048 | bytes 3268608 | tf_op jit(solution)/shard_map/abok,abo->abk/dot_general | solution.py:45
  136.7 4.4 %fusion.15 = f32[32,1,128]{2,1,0:T(1,128)S(1)} fusion(f32[32,128,1]{1,2,0:T(1,128)S(1)} %bitcast.76, f32[32,128,128]{2,0,1:T(8,128)S(1)} %copy_divide_fusion), kind=kOutput, calls=%fused_computation.27 | convolution fusion | flops 6291456 | bytes 2129920 | tf_op jit(solution)/shard_map/gkl,gl->gk/dot_general | solution.py:37
  141.9 2.3 %collective-permute-start.9 = (f32[1,4,128,128]{3,2,1,0:T(8,128)S(1)}, f32[1,4,128,128]{3,2,1,0:T(8,128)S(1)}, u32[]{:S(2)}, u32[]{:S(2)}) collective-permute-start(f32[1,4,128,128]{3,2,1,0:T(8,128)S(1)} %get-tuple-element.11), channel_id=1, source_target_pairs={{0,8},{8,16},{16,24},{24,0},{1,9},{9,17},{17,25},{25,1},{2,10},{10... | collective-permute-start | bytes 786440 | tf_op jit(solution)/shard_map/ppermute | solution.py:15
  146.7 5.2 %collective-permute-done.9 = f32[1,4,128,128]{3,2,1,0:T(8,128)S(1)} collective-permute-done((f32[1,4,128,128]{3,2,1,0:T(8,128)S(1)}, f32[1,4,128,128]{3,2,1,0:T(8,128)S(1)}, u32[]{:S(2)}, u32[]{:S(2)}) %collective-permute-start.9) | collective-permute-done | bytes 262176 | tf_op jit(solution)/shard_map/ppermute | solution.py:15
  152.0 3.7 %collective-permute-done.8 = f32[1,4,128,128]{3,2,1,0:T(8,128)S(1)} collective-permute-done((f32[1,4,128,128]{3,2,1,0:T(8,128)S(1)}, f32[1,4,128,128]{3,2,1,0:T(8,128)S(1)}, u32[]{:S(2)}, u32[]{:S(2)}) %collective-permute-start.8) | collective-permute-done | bytes 262176 | tf_op jit(solution)/shard_map/ppermute | solution.py:18
  159.1 13.2 %collective-permute-done.10 = f32[10,1,128,128]{2,3,1,0:T(8,128)S(1)} collective-permute-done((f32[10,1,128,128]{2,3,1,0:T(8,128)S(1)}, f32[10,1,128,128]{2,3,1,0:T(8,128)S(1)}, u32[]{:S(2)}, u32[]{:S(2)}) %collective-permute-start.10) | collective-permute-done | bytes 655392 | tf_op jit(solution)/shard_map/ppermute | solution.py:18
  172.3 2.9 %collective-permute-done.11 = f32[10,1,128,128]{2,3,1,0:T(8,128)S(1)} collective-permute-done((f32[10,1,128,128]{2,3,1,0:T(8,128)S(1)}, f32[10,1,128,128]{2,3,1,0:T(8,128)S(1)}, u32[]{:S(2)}, u32[]{:S(2)}) %collective-permute-start.11) | collective-permute-done | bytes 655392 | tf_op jit(solution)/shard_map/ppermute | solution.py:15
  175.2 6.8 %fusion.5 = bf16[8,4,512,128]{2,3,1,0:T(8,128)(2,1)} fusion(f32[8,4,512]{2,1,0:T(4,128)S(1)} %copy-done.5, bf16[8,4,512,128]{3,2,1,0:T(8,128)(2,1)} %param.8, f32[10,1,128,128]{2,3,1,0:T(8,128)S(1)} %collective-permute-done.11, f32[1,4,128,128]{2,3,1,0:T(8,128)S(1)} %copy.64, f32[8,4,128,128]{2,3,1,0:T(8,128)S(1)} %copy-done, ...), kind=kOutput, calls=%fused_computation.8 | convolution fusion | flops 548929536 | bytes 12386304 | tf_op jit(solution)/shard_map/abrk,abkm->abrm/dot_general | solution.py:101
  182.0 6.4 %copy.70 = bf16[8,4,512,128]{3,2,1,0:T(8,128)(2,1)} copy(bf16[8,4,512,128]{2,3,1,0:T(8,128)(2,1)} %fusion.5) | data formatting | bytes 8388608 | tf_op jit(solution)/shard_map/convert_element_type | solution.py:102
  (65 shorter events, 34.3 us)
Async XLA Ops:
  0.0 59.5 %copy-start.1 = (bf16[8,4,128,128]{3,2,1,0:T(8,128)(2,1)S(1)}, bf16[8,4,128,128]{3,2,1,0:T(8,128)(2,1)}, u32[]{:S(2)}) copy-start(bf16[8,4,128,128]{3,2,1,0:T(8,128)(2,1)} %param.10) | copy-start | bytes 3145732
  0.0 12.0 %copy-start.4 = (s32[8,4,12]{2,1,0:T(4,128)S(1)}, s32[8,4,12]{2,1,0:T(4,128)}, u32[]{:S(2)}) copy-start(s32[8,4,12]{2,1,0:T(4,128)} %param.14) | copy-start | bytes 4612
  0.0 12.2 %copy-start.3 = (f32[8,4,12]{2,1,0:T(4,128)S(1)}, f32[8,4,12]{2,1,0:T(4,128)}, u32[]{:S(2)}) copy-start(f32[8,4,12]{2,1,0:T(4,128)} %param.15) | copy-start | bytes 4612
  4.9 58.6 %collective-permute-start.4 = (bf16[2,4,2,128]{3,1,0,2:T(4,128)(2,1)S(1)}, bf16[2,4,2,128]{3,1,0,2:T(4,128)(2,1)S(1)}, u32[]{:S(2)}, u32[]{:S(2)}) collective-permute-start(bf16[2,4,2,128]{3,1,0,2:T(4,128)(2,1)S(1)} %get-tuple-element.21), channel_id=1, source_target_pairs={{0,8},{8,16},{16,24},{24,0},{1,9},{9,17},{17,25},{25,1},{2,10},{10... | collective-permute-start | bytes 12296 | tf_op jit(solution)/shard_map/ppermute | solution.py:15
  7.9 55.6 %collective-permute-start.5 = (bf16[2,4,2,128]{3,1,0,2:T(4,128)(2,1)S(1)}, bf16[2,4,2,128]{3,1,0,2:T(4,128)(2,1)S(1)}, u32[]{:S(2)}, u32[]{:S(2)}) collective-permute-start(bf16[2,4,2,128]{3,1,0,2:T(4,128)(2,1)S(1)} %get-tuple-element.22), channel_id=1, source_target_pairs={{8,0},{16,8},{24,16},{0,24},{9,1},{17,9},{25,17},{1,25},{10,2},{18... | collective-permute-start | bytes 12296 | tf_op jit(solution)/shard_map/ppermute | solution.py:18
  10.0 49.7 %collective-permute-start.1 = (bf16[2,4,128,128]{3,2,1,0:T(8,128)(2,1)S(1)}, bf16[2,4,128,128]{3,2,1,0:T(8,128)(2,1)S(1)}, u32[]{:S(2)}, u32[]{:S(2)}) collective-permute-start(bf16[2,4,128,128]{3,2,1,0:T(8,128)(2,1)S(1)} %get-tuple-element.15), channel_id=1, source_target_pairs={{8,0},{16,8},{24,16},{0,24},{9,1},{17,9},{25,17},{1,25},{10,2},{18... | collective-permute-start | bytes 786440 | tf_op jit(solution)/shard_map/ppermute | solution.py:18
  12.0 47.5 %collective-permute-start = (bf16[2,4,128,128]{3,2,1,0:T(8,128)(2,1)S(1)}, bf16[2,4,128,128]{3,2,1,0:T(8,128)(2,1)S(1)}, u32[]{:S(2)}, u32[]{:S(2)}) collective-permute-start(bf16[2,4,128,128]{3,2,1,0:T(8,128)(2,1)S(1)} %get-tuple-element.16), channel_id=1, source_target_pairs={{0,8},{8,16},{16,24},{24,0},{1,9},{9,17},{17,25},{25,1},{2,10},{10... | collective-permute-start | bytes 786440 | tf_op jit(solution)/shard_map/ppermute | solution.py:15
  59.7 3.8 %copy-start.2 = (bf16[8,4,128]{2,1,0:T(4,128)(2,1)S(1)}, bf16[8,4,128]{2,1,0:T(4,128)(2,1)}, u32[]{:S(2)}) copy-start(bf16[8,4,128]{2,1,0:T(4,128)(2,1)} %param.12) | copy-start | bytes 24580
  59.9 22.0 %collective-permute-start.2 = (bf16[12,2,128,128]{3,2,1,0:T(8,128)(2,1)S(1)}, bf16[12,2,128,128]{3,2,1,0:T(8,128)(2,1)S(1)}, u32[]{:S(2)}, u32[]{:S(2)}) collective-permute-start(bf16[12,2,128,128]{3,2,1,0:T(8,128)(2,1)S(1)} %get-tuple-element.13), channel_id=1, source_target_pairs={{0,1},{1,2},{2,3},{3,4},{4,5},{5,6},{6,7},{7,0},{8,9},{9,10},{10,1... | collective-permute-start | bytes 2359304 | tf_op jit(solution)/shard_map/ppermute | solution.py:15
  59.9 22.0 %collective-permute-start.3 = (bf16[12,2,128,128]{3,2,1,0:T(8,128)(2,1)S(1)}, bf16[12,2,128,128]{3,2,1,0:T(8,128)(2,1)S(1)}, u32[]{:S(2)}, u32[]{:S(2)}) collective-permute-start(bf16[12,2,128,128]{3,2,1,0:T(8,128)(2,1)S(1)} %get-tuple-element.14), channel_id=1, source_target_pairs={{1,0},{2,1},{3,2},{4,3},{5,4},{6,5},{7,6},{0,7},{9,8},{10,9},{11,1... | collective-permute-start | bytes 2359304 | tf_op jit(solution)/shard_map/ppermute | solution.py:18
  63.5 18.3 %collective-permute-start.6 = (bf16[12,2,2,128]{3,1,0,2:T(2,128)(2,1)S(1)}, bf16[12,2,2,128]{3,1,0,2:T(2,128)(2,1)S(1)}, u32[]{:S(2)}, u32[]{:S(2)}) collective-permute-start(bf16[12,2,2,128]{3,1,0,2:T(2,128)(2,1)S(1)} %get-tuple-element.19), channel_id=1, source_target_pairs={{0,1},{1,2},{2,3},{3,4},{4,5},{5,6},{6,7},{7,0},{8,9},{9,10},{10,1... | collective-permute-start | bytes 36872 | tf_op jit(solution)/shard_map/ppermute | solution.py:15
  63.6 18.2 %collective-permute-start.7 = (bf16[12,2,2,128]{3,1,0,2:T(2,128)(2,1)S(1)}, bf16[12,2,2,128]{3,1,0,2:T(2,128)(2,1)S(1)}, u32[]{:S(2)}, u32[]{:S(2)}) collective-permute-start(bf16[12,2,2,128]{3,1,0,2:T(2,128)(2,1)S(1)} %get-tuple-element.20), channel_id=1, source_target_pairs={{1,0},{2,1},{3,2},{4,3},{5,4},{6,5},{7,6},{0,7},{9,8},{10,9},{11,1... | collective-permute-start | bytes 36872 | tf_op jit(solution)/shard_map/ppermute | solution.py:18
  141.9 10.0 %collective-permute-start.9 = (f32[1,4,128,128]{3,2,1,0:T(8,128)S(1)}, f32[1,4,128,128]{3,2,1,0:T(8,128)S(1)}, u32[]{:S(2)}, u32[]{:S(2)}) collective-permute-start(f32[1,4,128,128]{3,2,1,0:T(8,128)S(1)} %get-tuple-element.11), channel_id=1, source_target_pairs={{0,8},{8,16},{16,24},{24,0},{1,9},{9,17},{17,25},{25,1},{2,10},{10... | collective-permute-start | bytes 786440 | tf_op jit(solution)/shard_map/ppermute | solution.py:15
  144.2 11.5 %collective-permute-start.8 = (f32[1,4,128,128]{3,2,1,0:T(8,128)S(1)}, f32[1,4,128,128]{3,2,1,0:T(8,128)S(1)}, u32[]{:S(2)}, u32[]{:S(2)}) collective-permute-start(f32[1,4,128,128]{3,2,1,0:T(8,128)S(1)} %get-tuple-element.12), channel_id=1, source_target_pairs={{8,0},{16,8},{24,16},{0,24},{9,1},{17,9},{25,17},{1,25},{10,2},{18... | collective-permute-start | bytes 786440 | tf_op jit(solution)/shard_map/ppermute | solution.py:18
  155.8 19.4 %copy-start = (f32[8,4,128,128]{2,3,1,0:T(8,128)S(1)}, f32[8,4,128,128]{2,3,1,0:T(8,128)}, u32[]{:S(2)}) copy-start(f32[8,4,128,128]{2,3,1,0:T(8,128)} %copy.62) | copy-start | bytes 6291460
  155.9 19.4 %copy-start.5 = (f32[8,4,512]{2,1,0:T(4,128)S(1)}, f32[8,4,512]{2,1,0:T(4,128)}, u32[]{:S(2)}) copy-start(f32[8,4,512]{2,1,0:T(4,128)} %param.9) | copy-start | bytes 196612
  157.3 15.0 %collective-permute-start.10 = (f32[10,1,128,128]{2,3,1,0:T(8,128)S(1)}, f32[10,1,128,128]{2,3,1,0:T(8,128)S(1)}, u32[]{:S(2)}, u32[]{:S(2)}) collective-permute-start(f32[10,1,128,128]{2,3,1,0:T(8,128)S(1)} %get-tuple-element.9), channel_id=1, source_target_pairs={{1,0},{2,1},{3,2},{4,3},{5,4},{6,5},{7,6},{0,7},{9,8},{10,9},{11,1... | collective-permute-start | bytes 1966088 | tf_op jit(solution)/shard_map/ppermute | solution.py:18
  159.1 16.1 %collective-permute-start.11 = (f32[10,1,128,128]{2,3,1,0:T(8,128)S(1)}, f32[10,1,128,128]{2,3,1,0:T(8,128)S(1)}, u32[]{:S(2)}, u32[]{:S(2)}) collective-permute-start(f32[10,1,128,128]{2,3,1,0:T(8,128)S(1)} %get-tuple-element.10), channel_id=1, source_target_pairs={{0,1},{1,2},{2,3},{3,4},{4,5},{5,6},{6,7},{7,0},{8,9},{9,10},{10,1... | collective-permute-start | bytes 1966088 | tf_op jit(solution)/shard_map/ppermute | solution.py:15
where the time goes:
time: 192 us; the launch traced here: 189 us
  matrix products  64.1 us (33%)
  blocking collectives  45.6 us (24%)
  waiting for transfers between devices  39.7 us (21%)
  starting transfers between devices  18 us (9%)
  local copies, waits for them, and re-layouts  11.1 us (6%)
  other arithmetic  8.26 us (4%)
  between operations  1.92 us (1%)
    psum x1, blocking collectives, shards(): lax.psum((jnp.sum(obs_weight * innov_f * innov_f), jnp.sum(live_slot.asty...  45.6 us
    ppermute x6, waiting for transfers between devices, with_halo(): lax.ppermute(lax.slice_in_dim(block, block.shape[dim] - width, None, axis...  22.7 us
    ppermute x6, waiting for transfers between devices, with_halo(): lax.ppermute(lax.slice_in_dim(block, 0, width, axis=dim), axis, backward)  16.9 us
    ppermute x6, starting transfers between devices, with_halo(): lax.ppermute(lax.slice_in_dim(block, 0, width, axis=dim), axis, backward)  12.5 us
    dot_general x5, matrix products, transform(): jnp.einsum('gkl,glm->gkm', inv_iter, root_iter, precision=lax.Precision.H...  12.4 us
    dot_general x5, matrix products, transform(): jnp.einsum('gkl,glm->gkm', update, inv_iter, precision=lax.Precision.HIGH...  11.6 us
    dot_general x4, matrix products, transform(): jnp.einsum('gkl,glm->gkm', root_iter, update, precision=lax.Precision.HIG...  10.9 us
    dot_general x1, matrix products, group_weights(): jnp.dot(picker, grams.reshape(outer_x * outer_y, width * width), precisio...  6.82 us
  transfers between devices with their start and end apart: 12, of which 5 were waited for; matrix products, arithmetic and copies ran while one was open for 2% of the time, Pallas kernels for 0%

commit v1 on v0

v1 whole, which is shorter than its diff:
```python
import functools
import math

import jax
import jax.numpy as jnp
from jax import lax
from jax.experimental import pallas as pl
from jax.experimental.pallas import tpu as pltpu
from jax.sharding import PartitionSpec as P

MESH = pl.DeviceIdType.MESH
HALO = 2
F32 = jnp.float32
BF16 = jnp.bfloat16


def offsets(nx, ny):
    found = {(dx, 0) for dx in range(1, nx)} | {(0, dy) for dy in range(1, ny)}
    found |= {(dx % nx, dy % ny) for dx in (-1, 1) for dy in (-1, 1)}
    return sorted(found - {(0, 0)})


def product(left, right):
    s, a = left
    t, b = right
    cross = jnp.dot(a.astype(BF16), b.astype(BF16), preferred_element_type=F32)
    return s * t, cross + (s * b + t * a)


def two_sweeps(y):
    s = [product(v, v) for v in y]
    inner = [
        (0.0625 * q[0] - 0.5625 * v[0] + 1.6875, 0.0625 * q[1] - 0.5625 * v[1])
        for q, v in zip(s, y)
    ]
    h = [product(q, i) for q, i in zip(s, inner)]
    return [(p[0] - 2.4375 * v[0] + 2.25, p[1] - 2.4375 * v[1]) for p, v in zip(h, y)]


def analysis_weights(nx, ny, cnt, nb, lw, pert, rinv, innov, out,
                     grams, wts, wsend, htx, hty, st_own, st_x, st_sum, st_y,
                     g_send, g_recv, x_send, x_recv, y_send, y_recv, w_send, w_recv):
    na, nbk, slots, width = pert.shape
    listed = nb.shape[2]
    half = width // 2
    mx, my = lax.axis_index("tx"), lax.axis_index("ty")

    def at(dx, dy):
        return {"tx": lax.rem(mx + (dx % nx), nx), "ty": lax.rem(my + (dy % ny), ny)}

    barrier = pltpu.get_barrier_semaphore()
    partners = offsets(nx, ny)
    for dx, dy in partners:
        pl.semaphore_signal(barrier, inc=1, device_id=at(dx, dy), device_id_type=MESH)

    lane = lax.broadcasted_iota(jnp.int32, (1, slots), 1)
    eye = (lax.broadcasted_iota(jnp.int32, (width, width), 0)
           == lax.broadcasted_iota(jnp.int32, (width, width), 1))
    hrow = lax.broadcasted_iota(jnp.int32, (half, width), 0)
    hlane = lax.broadcasted_iota(jnp.int32, (half, width), 1)

    def gram_row(a, sums):
        first, second = sums
        for b in range(nbk):
            p = pert[a, b]
            live = lane < cnt[a, b]
            q = jnp.where(live, rinv[a, b:b + 1, :].astype(F32), 0.0)
            d = innov[a, b:b + 1, :].astype(F32)
            qd = q * d
            hi = qd.astype(BF16)
            lo = (qd - hi.astype(F32)).astype(BF16)
            scaled = (jnp.transpose(p.astype(F32)) * q).astype(BF16)
            sub = lax.broadcasted_iota(jnp.int32, (16, slots), 0)
            tail = jnp.where(sub == 0, hi.astype(F32), jnp.where(sub == 1, lo.astype(F32), 0.0))
            g = jnp.dot(scaled, p, preferred_element_type=F32)
            v = jnp.dot(tail.astype(BF16), p, preferred_element_type=F32)
            diag = jnp.sum(jnp.where(eye, g, 0.0), axis=0, keepdims=True)
            first = first + qd * d
            second = second + (jnp.where(live, 1.0, 0.0) + diag * (1.0 / (width - 1)))
            lower = pltpu.roll(g[half:], half, 1)
            packed = jnp.where(hrow <= hlane, g[:half], lower)
            vec = v[0:1] + v[1:2]
            vhi = vec.astype(BF16).astype(F32)
            subw = lax.broadcasted_iota(jnp.int32, (16, width), 0)
            extra = jnp.where(subw == 0, diag,
                              jnp.where(subw == 1, vhi, jnp.where(subw == 2, vec - vhi, 0.0)))
            grams[a + HALO, b + HALO, :half, :] = packed.astype(BF16)
            grams[a + HALO, b + HALO, half:, :] = extra.astype(BF16)
        return first, second

    def span(step, n):
        if step == 0:
            return pl.ds(HALO, n), pl.ds(HALO, n)
        if step == 1:
            return pl.ds(n, HALO), pl.ds(0, HALO)
        return pl.ds(HALO, HALO), pl.ds(n + HALO, HALO)

    def halo_copy(k, dx, dy):
        sa, da = span(dx, na)
        sb, db = span(dy, nbk)
        return pltpu.make_async_remote_copy(
            src_ref=grams.at[sa, sb], dst_ref=grams.at[da, db],
            send_sem=g_send.at[k], recv_sem=g_recv.at[k],
            device_id=at(dx, dy), device_id_type=MESH)

    early = [(1, 0), (-1, 0), (1, 1), (1, -1), (-1, 1), (-1, -1)]
    late = [(0, 1), (0, -1)]
    zero = jnp.zeros((1, slots), F32)
    sums = lax.fori_loop(
        0, 2 * HALO, lambda i, s: gram_row(i + (na - 2 * HALO) * (i // HALO), s), (zero, zero))
    pl.semaphore_wait(barrier, len(partners))
    copies = [halo_copy(k, dx, dy) for k, (dx, dy) in enumerate(early)]
    for c in copies:
        c.start()
    sums = lax.fori_loop(HALO, na - HALO, gram_row, sums)
    more = [halo_copy(len(early) + k, dx, dy) for k, (dx, dy) in enumerate(late)]
    for c in more:
        c.start()
    copies += more

    rows8 = lax.broadcasted_iota(jnp.int32, (8, slots), 0)
    st_own[...] = jnp.where(rows8 == 0, sums[0], jnp.where(rows8 == 1, sums[1], 0.0))
    xs = [pltpu.make_async_remote_copy(
        src_ref=st_own, dst_ref=st_x.at[k - 1], send_sem=x_send.at[k - 1],
        recv_sem=x_recv.at[k - 1], device_id=at(k, 0), device_id_type=MESH)
        for k in range(1, nx)]
    for c in xs:
        c.start()
    for c in xs:
        c.wait_recv()
    st_sum[...] = st_own[...] + jnp.sum(st_x[...], axis=0)
    ys = [pltpu.make_async_remote_copy(
        src_ref=st_sum, dst_ref=st_y.at[k - 1], send_sem=y_send.at[k - 1],
        recv_sem=y_recv.at[k - 1], device_id=at(0, k), device_id_type=MESH)
        for k in range(1, ny)]
    for c in ys:
        c.start()
    for c in ys:
        c.wait_recv()
    total = jnp.sum(st_sum[...] + jnp.sum(st_y[...], axis=0), axis=1, keepdims=True)
    inflation = (width - 1) * total[1:2] / total[0:1]
    for c in copies:
        c.wait_recv()

    def listed_sum(a, b):
        acc = None
        for j in range(listed):
            code = nb[a, b, j]
            down = lax.shift_right_logical(code * 13, 6)
            block = grams[a + down, b + (code - 5 * down)].astype(F32)
            term = lw[a, b, j] * block
            acc = term if acc is None else acc + term
        return acc

    def unpack(acc):
        c = acc[:half]
        diag = acc[half:half + 1]
        vec = acc[half + 1:half + 2] + acc[half + 2:half + 3]
        flipped = jnp.transpose(jnp.concatenate([c, c], axis=0))
        top = jnp.where(hrow <= hlane, c, flipped[:half])
        shifted = pltpu.roll(c, half, 1)
        column = hlane - half
        square = jnp.where(hrow > column, shifted, jnp.where(hrow == column, diag, flipped[:half]))
        bottom = jnp.where(column < 0, flipped[half:], square)
        return jnp.concatenate([top, bottom], axis=0), vec

    def transform(groups, send):
        pairs = [unpack(listed_sum(a, b)) for a, b in groups]
        vecs = [v for _, v in pairs]
        ms = [jnp.where(eye, m + inflation, m) for m, _ in pairs]
        inv = [lax.rsqrt(jnp.sum(jnp.sum(m * m, axis=0, keepdims=True), axis=1, keepdims=True))
               for m in ms]
        mid = [jnp.sum(jnp.sum(jnp.where(eye, m, 0.0), axis=0, keepdims=True), axis=1,
                       keepdims=True) * (1.0 / width) for m in ms]
        y = [(c * i, jnp.where(eye, m - c, m) * i) for m, i, c in zip(ms, inv, mid)]
        z2 = two_sweeps(y)
        t2 = [product(v, product(z, z)) for v, z in zip(y, z2)]
        w = two_sweeps(t2)
        z4 = [product(z, u) for z, u in zip(z2, w)]
        t4 = [product(t, product(u, u)) for t, u in zip(t2, w)]
        z5 = [product(z, (1.5 - 0.5 * t[0], -0.5 * t[1])) for z, t in zip(z4, t4)]
        for (a, b), (z, r), v, i in zip(groups, z5, vecs, inv):
            rb = r.astype(BF16)
            x = jnp.broadcast_to(v, (16, width))
            for _ in range(2):
                x = z * x + jnp.dot(x.astype(BF16), rb, preferred_element_type=F32)
            shift = jnp.transpose(jnp.broadcast_to(x[0:1] * i, (width, width)))
            scale = math.sqrt(width - 1) * jnp.sqrt(i)
            weight = scale * jnp.where(eye, r + z, r) + shift
            wts[a, b] = weight
            if send:
                wsend[a, b] = weight.astype(BF16)

    def w_copy(k, src, dst, dx, dy):
        return pltpu.make_async_remote_copy(
            src_ref=src, dst_ref=dst, send_sem=w_send.at[k], recv_sem=w_recv.at[k],
            device_id=at(dx, dy), device_id_type=MESH)

    @pl.loop(0, 2)
    def _(i):
        transform([(i * (na - 1), b) for b in range(nbk)], True)

    wx = [w_copy(0, wsend.at[na - 1], htx.at[0], 1, 0), w_copy(1, wsend.at[0], htx.at[1], -1, 0)]
    for c in wx:
        c.start()

    @pl.loop(0, (na - 2) // 2)
    def _(i):
        transform([(1 + 2 * i + k, b) for k in range(2) for b in (0, nbk - 1)], True)

    wy = [w_copy(2, wsend.at[:, nbk - 1], hty.at[0], 0, 1),
          w_copy(3, wsend.at[:, 0], hty.at[1], 0, -1)]
    for c in wy:
        c.start()

    @pl.loop(0, (na - 2) // 2)
    def _(i):
        transform([(1 + 2 * i + k, b) for k in range(2) for b in range(1, nbk - 1)], False)

    def blend(a, b, lower, upper):
        left = wts[a, b - 1] if b > 0 else hty[0, a].astype(F32)
        right = wts[a, b + 1] if b < nbk - 1 else hty[1, a].astype(F32)
        out[a, b] = ((4.0 * wts[a, b] + (upper + lower) + (left + right)) * 0.125).astype(BF16)

    @pl.loop(1, na - 1)
    def _(a):
        for b in range(1, nbk - 1):
            blend(a, b, wts[a - 1, b], wts[a + 1, b])

    for c in wx:
        c.wait_recv()
    for c in wy:
        c.wait_recv()

    @pl.loop(1, na - 1)
    def _(a):
        for b in (0, nbk - 1):
            blend(a, b, wts[a - 1, b], wts[a + 1, b])

    for b in range(nbk):
        blend(0, b, htx[0, b].astype(F32), wts[1, b])
        blend(na - 1, b, wts[na - 2, b], htx[1, b].astype(F32))
    for c in copies + xs + ys + wx + wy:
        c.wait_send()


def apply_weights(members, mean, blended, out):
    for b in range(members.shape[1]):
        base = jnp.transpose(jnp.broadcast_to(mean[0, b:b + 1, :], (8, mean.shape[2])))[:, 0:1]
        value = jnp.dot(members[0, b], blended[0, b], preferred_element_type=F32)
        out[0, b] = (value + base).astype(BF16)


def shards(nx, ny, members, mean_state, obs_pert, obs_rinv, innovation, obs_count, neighbours,
           loc_weight):
    na, nbk, slots, width = obs_pert.shape
    smem = pl.BlockSpec(memory_space=pltpu.SMEM)
    vmem = pl.BlockSpec(memory_space=pltpu.VMEM)
    dma = pltpu.SemaphoreType.DMA
    half = width // 2
    blended = pl.pallas_call(
        functools.partial(analysis_weights, nx, ny),
        out_shape=jax.ShapeDtypeStruct((na, nbk, width, width), BF16),
        in_specs=[smem] * 3 + [vmem] * 3,
        out_specs=vmem,
        scratch_shapes=[
            pltpu.VMEM((na + 2 * HALO, nbk + 2 * HALO, half + 16, width), BF16),
            pltpu.VMEM((na, nbk, width, width), F32),
            pltpu.VMEM((na, nbk, width, width), BF16),
            pltpu.VMEM((2, nbk, width, width), BF16),
            pltpu.VMEM((2, na, width, width), BF16),
            pltpu.VMEM((8, slots), F32),
            pltpu.VMEM((nx - 1, 8, slots), F32),
            pltpu.VMEM((8, slots), F32),
            pltpu.VMEM((ny - 1, 8, slots), F32),
            dma((8,)), dma((8,)),
            dma((nx - 1,)), dma((nx - 1,)),
            dma((ny - 1,)), dma((ny - 1,)),
            dma((4,)), dma((4,)),
        ],
        compiler_params=pltpu.CompilerParams(
            collective_id=0, has_side_effects=True, vmem_limit_bytes=40 * 1024 * 1024),
    )(obs_count, neighbours, loc_weight, obs_pert, obs_rinv, innovation)
    levels = members.shape[2]
    return pl.pallas_call(
        apply_weights,
        grid=(na,),
        out_shape=jax.ShapeDtypeStruct(members.shape, BF16),
        in_specs=[
            pl.BlockSpec((1, nbk, levels, width), lambda i: (i, 0, 0, 0)),
            pl.BlockSpec((1, nbk, levels), lambda i: (i, 0, 0)),
            pl.BlockSpec((1, nbk, width, width), lambda i: (i, 0, 0, 0)),
        ],
        out_specs=pl.BlockSpec((1, nbk, levels, width), lambda i: (i, 0, 0, 0)),
        compiler_params=pltpu.CompilerParams(vmem_limit_bytes=32 * 1024 * 1024),
    )(members, mean_state, blended)


def solution(mesh):
    nx, ny = mesh.shape["tx"], mesh.shape["ty"]
    return jax.shard_map(
        functools.partial(shards, nx, ny),
        mesh=mesh,
        in_specs=(
            P("tx", "ty", None, None),
            P("tx", "ty", None),
            P("tx", "ty", None, None),
            P("tx", "ty", None),
            P("tx", "ty", None),
            P("tx", "ty"),
            P("tx", "ty", None),
            P("tx", "ty", None),
        ),
        out_specs=P("tx", "ty", None, None),
        check_vma=False,
    )
```

time: 192 us -> 62.1 us (0.32); the launches traced: 189 us -> 61.6 us
  matrix products: 64.1 us -> 0 us
  Pallas kernels: 0 us -> 53.7 us
  blocking collectives: 45.6 us -> 0 us
  waiting for transfers between devices: 39.7 us -> 0 us
  starting transfers between devices: 18 us -> 0 us
  other arithmetic: 8.26 us -> 0 us
  local copies, waits for them, and re-layouts: 11.1 us -> 7.83 us
    dot_general x21 -> x0, matrix products: 64.1 us -> none  [the longest x5 12.4 us: transform(): jnp.einsum('gkl,glm->gkm', inv_iter, root_iter, precision=lax.Precision.H...]
    pallas_call x0 -> x2, Pallas kernels: none -> 53.7 us  [the longest x1 47.2 us: shards(): pl.pallas_call(functools.partial(analysis_weights, nx, ny), out_shape=jax...]
    psum x1 -> x0, blocking collectives: 45.6 us -> none  [shards(): lax.psum((jnp.sum(obs_weight * innov_f * innov_f), jnp.sum(live_slot.asty...]
    ppermute x12 -> x0, waiting for transfers between devices: 39.7 us -> none  [the longest x6 22.7 us: with_halo(): lax.ppermute(lax.slice_in_dim(block, block.shape[dim] - width, None, axis...]
    ppermute x12 -> x0, starting transfers between devices: 18 us -> none  [the longest x6 12.5 us: with_halo(): lax.ppermute(lax.slice_in_dim(block, 0, width, axis=dim), axis, backward)]
    unnamed x16 -> x15, local copies, waits for them, and re-layouts: 1.17 us -> 7.83 us
    convert_element_type x1 -> x0, local copies, waits for them, and re-layouts: 6.43 us -> none  [shards(): return (result + mean_state[..., None]).astype(jnp.bfloat16)]
    reduce_sum x3 -> x0, other arithmetic: 3.49 us -> none  [the longest x1 1.84 us: shards(): square_sum = jnp.sum(jnp.square(obs_pert.astype(jnp.float32)), axis=-1)]
  transfers between devices with their start and end apart: 12 -> 0, of which waited for: 5 -> 0; matrix products, arithmetic and copies ran while one was open for 2% -> 0% of each run, Pallas kernels for 0% -> 0%
where the time goes in v1:
time: 62.1 us; the launch traced here: 61.6 us
  Pallas kernels  53.7 us (86%)
  local copies, waits for them, and re-layouts  7.83 us (13%)
    pallas_call x1, Pallas kernels, shards(): pl.pallas_call(functools.partial(analysis_weights, nx, ny), out_shape=jax...  47.2 us
    unnamed x15, local copies, waits for them, and re-layouts  7.83 us
    pallas_call x1, Pallas kernels, shards(): pl.pallas_call(apply_weights, grid=(na,), out_shape=jax.ShapeDtypeStruct(...  6.52 us

profile of v1, /device:TPU:0, one launch (start us, length us, event | category | flops | bytes accessed | tf_op | source)
XLA Modules:
  0.0 61.6 jit_solution(12024596520051343427)
XLA Ops:
  0.0 0.8 %copy.9.cnt = s32[8,4]{1,0:T(8,128)S(1)} copy(s32[8,4]{0,1:T(4,128)} %param.13) | data formatting | bytes 256 | tf_op args[5]
  0.8 0.0 copy-start.1
  0.8 1.2 %copy-done.1 = bf16[8,4,128,128]{3,2,1,0:T(8,128)(2,1)S(1)} copy-done((bf16[8,4,128,128]{3,2,1,0:T(8,128)(2,1)S(1)}, bf16[8,4,128,128]{3,2,1,0:T(8,128)(2,1)}, u32[]{:S(2)}) %copy-start.1) | copy-done | bytes 1048600
  2.0 0.0 copy-start.3
  2.0 0.7 %copy-done.3 = s32[8,4,12]{2,1,0:T(4,128)S(1)} copy-done((s32[8,4,12]{2,1,0:T(4,128)S(1)}, s32[8,4,12]{2,1,0:T(4,128)}, u32[]{:S(2)}) %copy-start.3) | copy-done | bytes 1560
  2.7 0.0 copy-start.4
  2.7 0.7 %copy-done.4 = f32[8,4,12]{2,1,0:T(4,128)S(1)} copy-done((f32[8,4,12]{2,1,0:T(4,128)S(1)}, f32[8,4,12]{2,1,0:T(4,128)}, u32[]{:S(2)}) %copy-start.4) | copy-done | bytes 1560
  3.4 0.0 copy-start.5
  3.4 0.7 %copy-done.5 = bf16[8,4,128]{2,1,0:T(4,128)(2,1)S(1)} copy-done((bf16[8,4,128]{2,1,0:T(4,128)(2,1)S(1)}, bf16[8,4,128]{2,1,0:T(4,128)(2,1)}, u32[]{:S(2)}) %copy-start.5) | copy-done | bytes 8216
  4.1 0.0 copy-start.6
  4.1 0.7 %copy-done.6 = bf16[8,4,128]{2,1,0:T(4,128)(2,1)S(1)} copy-done((bf16[8,4,128]{2,1,0:T(4,128)(2,1)S(1)}, bf16[8,4,128]{2,1,0:T(4,128)(2,1)}, u32[]{:S(2)}) %copy-start.6) | copy-done | bytes 8216
  4.8 47.2 %shard_map.82.blended = bf16[8,4,128,128]{3,2,1,0:T(8,128)(2,1)S(1)} custom-call(s32[8,4]{1,0:T(8,128)S(1)} %copy.9.cnt, s32[8,4,12]{2,1,0:T(4,128)S(1)} %copy-done.3, f32[8,4,12]{2,1,0:T(4,128)S(1)} %copy-done.4, bf16[8,4,128,128]{3,2,1,0:T(8,128)(2,1)S(1)} %copy-done.1, bf16[8,4,128]{2,1,0:T(4,128)(2,1)S(1)} %copy-done.5, bf16[8,4,128]{2,1,0:T(4,128)(2,1)S(1)} %copy-done.6), custom_call_target="tpu_custom_call" | custom-call | tf_op jit(solution)/shard_map/pallas_call | solution.py:261
  52.0 0.0 copy-start
  52.0 2.2 %copy-done = bf16[8,4,512,128]{3,2,1,0:T(8,128)(2,1)S(1)} copy-done((bf16[8,4,512,128]{3,2,1,0:T(8,128)(2,1)S(1)}, bf16[8,4,512,128]{3,2,1,0:T(8,128)(2,1)}, u32[]{:S(2)}) %copy-start) | copy-done | bytes 4194328
  54.2 0.0 copy-start.2
  54.2 0.8 %copy-done.2 = f32[8,4,512]{2,1,0:T(4,128)S(1)} copy-done((f32[8,4,512]{2,1,0:T(4,128)S(1)}, f32[8,4,512]{2,1,0:T(4,128)}, u32[]{:S(2)}) %copy-start.2) | copy-done | bytes 65560
  55.1 6.5 %shard_map.83 = bf16[8,4,512,128]{3,2,1,0:T(8,128)(2,1)} custom-call(bf16[8,4,512,128]{3,2,1,0:T(8,128)(2,1)S(1)} %copy-done, f32[8,4,512]{2,1,0:T(4,128)S(1)} %copy-done.2, bf16[8,4,128,128]{3,2,1,0:T(8,128)(2,1)S(1)} %shard_map.82.blended), custom_call_target="tpu_custom_call" | custom-call | tf_op jit(solution)/shard_map/pallas_call | solution.py:285
Async XLA Ops:
  0.8 1.2 %copy-start.1 = (bf16[8,4,128,128]{3,2,1,0:T(8,128)(2,1)S(1)}, bf16[8,4,128,128]{3,2,1,0:T(8,128)(2,1)}, u32[]{:S(2)}) copy-start(bf16[8,4,128,128]{3,2,1,0:T(8,128)(2,1)} %pert.1) | copy-start | bytes 3145732
  2.0 0.7 %copy-start.3 = (s32[8,4,12]{2,1,0:T(4,128)S(1)}, s32[8,4,12]{2,1,0:T(4,128)}, u32[]{:S(2)}) copy-start(s32[8,4,12]{2,1,0:T(4,128)} %nb.1) | copy-start | bytes 4612
  2.7 0.7 %copy-start.4 = (f32[8,4,12]{2,1,0:T(4,128)S(1)}, f32[8,4,12]{2,1,0:T(4,128)}, u32[]{:S(2)}) copy-start(f32[8,4,12]{2,1,0:T(4,128)} %lw.1) | copy-start | bytes 4612
  3.4 0.7 %copy-start.5 = (bf16[8,4,128]{2,1,0:T(4,128)(2,1)S(1)}, bf16[8,4,128]{2,1,0:T(4,128)(2,1)}, u32[]{:S(2)}) copy-start(bf16[8,4,128]{2,1,0:T(4,128)(2,1)} %rinv.1) | copy-start | bytes 24580
  4.1 0.7 %copy-start.6 = (bf16[8,4,128]{2,1,0:T(4,128)(2,1)S(1)}, bf16[8,4,128]{2,1,0:T(4,128)(2,1)}, u32[]{:S(2)}) copy-start(bf16[8,4,128]{2,1,0:T(4,128)(2,1)} %innov.1) | copy-start | bytes 24580
  52.0 2.2 %copy-start = (bf16[8,4,512,128]{3,2,1,0:T(8,128)(2,1)S(1)}, bf16[8,4,512,128]{3,2,1,0:T(8,128)(2,1)}, u32[]{:S(2)}) copy-start(bf16[8,4,512,128]{3,2,1,0:T(8,128)(2,1)} %members.1) | copy-start | bytes 12582916
  54.2 0.8 %copy-start.2 = (f32[8,4,512]{2,1,0:T(4,128)S(1)}, f32[8,4,512]{2,1,0:T(4,128)}, u32[]{:S(2)}) copy-start(f32[8,4,512]{2,1,0:T(4,128)} %mean.1) | copy-start | bytes 196612

commit v2 on v1

v2 whole, which is shorter than its diff:
```python
import functools
import math

import jax
import jax.numpy as jnp
from jax import lax
from jax.experimental import pallas as pl
from jax.experimental.pallas import tpu as pltpu
from jax.sharding import PartitionSpec as P

MESH = pl.DeviceIdType.MESH
HALO = 2
F32 = jnp.float32
BF16 = jnp.bfloat16


def offsets(nx, ny):
    found = {(dx, 0) for dx in range(1, nx)} | {(0, dy) for dy in range(1, ny)}
    found |= {(dx % nx, dy % ny) for dx in (-1, 1) for dy in (-1, 1)}
    return sorted(found - {(0, 0)})


def matmul(a, b):
    return jnp.dot(a.astype(BF16), b.astype(BF16), preferred_element_type=F32)


def square(x):
    s, a = x
    return s * s, matmul(a, a) + (2.0 * s) * a


def product(left, right):
    s, a = left
    t, b = right
    return s * t, matmul(a, b) + (s * b + t * a)


def two_sweeps(y):
    sq = [square(v) for v in y]
    inner = [q[1] - 9.0 * v[1] for q, v in zip(sq, y)]
    cross = [matmul(q[1], i) for q, i in zip(sq, inner)]
    out = []
    for c, q, v in zip(cross, sq, y):
        mid = q[0] - 9.0 * v[0] + 27.0
        out.append((q[0] * mid - 39.0 * v[0] + 36.0,
                    c + ((mid + q[0]) * q[1] - (9.0 * q[0] + 39.0) * v[1])))
    return out


def scaled_by(x, factor):
    return x[0] * factor, x[1] * factor


def analysis_weights(nx, ny, cnt_h, nb_h, lw_h, pert_h, rinv_h, innov_h, mean_h,
                     out_h, mean_th,
                     out, mean_t, cnt, nb, lw, pert, rinv, innov, mean,
                     grams, landed, wts, wsend, htx, hty, st_own, st_x, st_sum, st_y,
                     i_sem, p_sem, o_sem, g_send, g_recv, x_send, x_recv, y_send, y_recv,
                     w_send, w_recv):
    na, nbk, slots, width = pert.shape
    listed = nb.shape[2]
    half = width // 2
    mx, my = lax.axis_index("tx"), lax.axis_index("ty")

    def at(dx, dy):
        return {"tx": lax.rem(mx + (dx % nx), nx), "ty": lax.rem(my + (dy % ny), ny)}

    barrier = pltpu.get_barrier_semaphore()
    partners = offsets(nx, ny)
    for dx, dy in partners:
        pl.semaphore_signal(barrier, inc=1, device_id=at(dx, dy), device_id_type=MESH)

    def pair_at(i):
        h = i // 2
        return (1 - h) * (na - 2) * i + h * 2 * (i - 1)

    loads = [pltpu.make_async_copy(src, dst, i_sem.at[k]) for k, (src, dst) in enumerate([
        (cnt_h, cnt), (rinv_h, rinv), (innov_h, innov), (nb_h, nb), (lw_h, lw), (mean_h, mean)])]
    for c in loads[:3]:
        c.start()

    def pert_load(i):
        rows = pl.ds(pair_at(i), 2)
        return pltpu.make_async_copy(pert_h.at[rows], pert.at[rows], p_sem.at[i])

    for i in range(na // 2):
        pert_load(i).start()
    for c in loads[3:]:
        c.start()
    for c in loads[:3]:
        c.wait()

    lane = lax.broadcasted_iota(jnp.int32, (1, slots), 1)
    eye = (lax.broadcasted_iota(jnp.int32, (width, width), 0)
           == lax.broadcasted_iota(jnp.int32, (width, width), 1))
    hrow = lax.broadcasted_iota(jnp.int32, (half, width), 0)
    hlane = lax.broadcasted_iota(jnp.int32, (half, width), 1)
    sub = lax.broadcasted_iota(jnp.int32, (16, slots), 0)
    subw = lax.broadcasted_iota(jnp.int32, (16, width), 0)

    def gram_terms(a, b):
        p = pert[a, b]
        live = lane < cnt[b, a]
        q = jnp.where(live, rinv[a, b:b + 1, :].astype(F32), 0.0)
        d = innov[a, b:b + 1, :].astype(F32)
        qd = q * d
        hi = qd.astype(BF16).astype(F32)
        scaled = (jnp.transpose(p.astype(F32)) * q).astype(BF16)
        tail = jnp.where(sub == 0, hi, jnp.where(sub == 1, qd - hi, 0.0))
        g = jnp.dot(scaled, p, preferred_element_type=F32)
        v = jnp.dot(tail.astype(BF16), p, preferred_element_type=F32)
        diag = jnp.sum(jnp.where(eye, g, 0.0), axis=0, keepdims=True)
        lower = pltpu.roll(g[half:], half, 1)
        packed = jnp.where(hrow <= hlane, g[:half], lower)
        vec = v[0:1] + v[1:2]
        vhi = vec.astype(BF16).astype(F32)
        extra = jnp.where(subw == 0, diag,
                          jnp.where(subw == 1, vhi, jnp.where(subw == 2, vec - vhi, 0.0)))
        grams[a + HALO, b + HALO, :half, :] = packed.astype(BF16)
        grams[a + HALO, b + HALO, half:, :] = extra.astype(BF16)
        return qd * d, jnp.where(live, 1.0, 0.0) + diag * (1.0 / (width - 1))

    def span(step, n):
        if step == 0:
            return pl.ds(HALO, n), pl.ds(HALO, n)
        if step == 1:
            return pl.ds(n, HALO), pl.ds(0, HALO)
        return pl.ds(HALO, HALO), pl.ds(n + HALO, HALO)

    def halo_copy(k):
        dx, dy = directions[k]
        sa, da = span(dx, na)
        sb, db = span(dy, nbk)
        target = grams.at[da, db] if dx == 0 else landed.at[(1 - dx) // 2, :, db]
        return pltpu.make_async_remote_copy(
            src_ref=grams.at[sa, sb], dst_ref=target,
            send_sem=g_send.at[k], recv_sem=g_recv.at[k],
            device_id=at(dx, dy), device_id_type=MESH)

    directions = [(1, 0), (-1, 0), (0, 1), (0, -1), (1, 1), (1, -1), (-1, 1), (-1, -1)]

    def gram_rows(i, sums):
        first, second = sums
        pert_load(i).wait()
        base = pair_at(i)
        for k in range(2):
            for b in range(nbk):
                one, two = gram_terms(base + k, b)
                first, second = first + one, second + two

        @pl.when(i == 1)
        def _():
            pl.semaphore_wait(barrier, len(partners))
            for k in (0, 1):
                halo_copy(k).start()

        return first, second

    zero = jnp.zeros((1, slots), F32)
    sums = lax.fori_loop(0, na // 2, gram_rows, (zero, zero))
    rows8 = lax.broadcasted_iota(jnp.int32, (8, slots), 0)
    st_own[...] = jnp.where(rows8 == 0, sums[0], jnp.where(rows8 == 1, sums[1], 0.0))
    xs = [pltpu.make_async_remote_copy(
        src_ref=st_own, dst_ref=st_x.at[k - 1], send_sem=x_send.at[k - 1],
        recv_sem=x_recv.at[k - 1], device_id=at(k, 0), device_id_type=MESH)
        for k in range(1, nx)]
    for c in xs:
        c.start()
    for k in range(2, 8):
        halo_copy(k).start()

    loads[5].wait()

    @pl.loop(0, na)
    def _(a):
        row = mean[a]
        high = row.astype(BF16).astype(F32)
        rest = row - high
        middle = rest.astype(BF16).astype(F32)
        fill = jnp.zeros((width - 3 * nbk, row.shape[1]), F32)
        stack = jnp.concatenate([high, middle, rest - middle, fill], axis=0)
        mean_t[a] = jnp.transpose(stack).astype(BF16)

    mean_out = pltpu.make_async_copy(mean_t, mean_th, i_sem.at[6])
    mean_out.start()

    for c in xs:
        c.wait_recv()
    st_sum[...] = st_own[...] + jnp.sum(st_x[...], axis=0)
    ys = [pltpu.make_async_remote_copy(
        src_ref=st_sum, dst_ref=st_y.at[k - 1], send_sem=y_send.at[k - 1],
        recv_sem=y_recv.at[k - 1], device_id=at(0, k), device_id_type=MESH)
        for k in range(1, ny)]
    for c in ys:
        c.start()
    loads[3].wait()
    loads[4].wait()
    for c in ys:
        c.wait_recv()
    total = jnp.sum(st_sum[...] + jnp.sum(st_y[...], axis=0), axis=1, keepdims=True)
    inflation = (width - 1) * total[1:2] / total[0:1]
    for k in (2, 3):
        halo_copy(k).wait_recv()

    def listed_sum(a, b):
        acc = None
        for j in range(listed):
            code = nb[a, b, j]
            down = lax.shift_right_logical(code * 13, 6)
            block = grams[a + down, b + (code - 5 * down)].astype(F32)
            term = lw[a, b, j] * block
            acc = term if acc is None else acc + term
        return acc

    def unpack(acc):
        c = acc[:half]
        diag = acc[half:half + 1]
        vec = acc[half + 1:half + 2] + acc[half + 2:half + 3]
        flipped = jnp.transpose(jnp.concatenate([c, c], axis=0))
        top = jnp.where(hrow <= hlane, c, flipped[:half])
        shifted = pltpu.roll(c, half, 1)
        column = hlane - half
        corner = jnp.where(hrow > column, shifted, jnp.where(hrow == column, diag, flipped[:half]))
        bottom = jnp.where(column < 0, flipped[half:], corner)
        return jnp.concatenate([top, bottom], axis=0), vec

    def total_of(m):
        return jnp.sum(jnp.sum(m, axis=0, keepdims=True), axis=1, keepdims=True)

    def transform(groups):
        pairs = [unpack(listed_sum(a, b)) for a, b in groups]
        vecs = [v for _, v in pairs]
        ms = [jnp.where(eye, m + inflation, m) for m, _ in pairs]
        inv = [lax.rsqrt(total_of(m * m)) for m in ms]
        mid = [total_of(jnp.where(eye, m, 0.0)) * (1.0 / width) for m in ms]
        y = [(c * i, jnp.where(eye, m - c, m) * i) for m, i, c in zip(ms, inv, mid)]
        z2 = two_sweeps(y)
        v2 = [square(z) for z in z2]
        t2 = [scaled_by(product(p, v), 1.0 / 256) for p, v in zip(y, v2)]
        w = two_sweeps(t2)
        z4 = [product(z, u) for z, u in zip(z2, w)]
        v4 = [square(u) for u in w]
        t4 = [product(t, v) for t, v in zip(t2, v4)]
        z5 = [(z[0] * (768.0 - t[0]), (768.0 - t[0]) * z[1] - z[0] * t[1] - matmul(z[1], t[1]))
              for z, t in zip(z4, t4)]
        back = 1.0 / (256 * 512)
        z5 = [scaled_by(z, back) for z in z5]
        rb = [z[1].astype(BF16) for z in z5]
        x = [jnp.broadcast_to(v, (16, width)) for v in vecs]
        for _ in range(2):
            x = [z[0] * u + jnp.dot(u.astype(BF16), r, preferred_element_type=F32)
                 for z, u, r in zip(z5, x, rb)]
        shifts = [jnp.transpose(jnp.broadcast_to(u[0:1] * i, (width, width)))
                  for u, i in zip(x, inv)]
        for (a, b), (z, r), shift, i in zip(groups, z5, shifts, inv):
            scale = math.sqrt(width - 1) * jnp.sqrt(i)
            weight = scale * jnp.where(eye, r + z, r) + shift
            wts[a, b] = weight
            if b in (0, nbk - 1):
                wsend[a, b] = weight.astype(BF16)

    def w_copy(k, src, dst, dx, dy):
        return pltpu.make_async_remote_copy(
            src_ref=src, dst_ref=dst, send_sem=w_send.at[k], recv_sem=w_recv.at[k],
            device_id=at(dx, dy), device_id_type=MESH)

    def wx_copies():
        return [w_copy(0, wsend.at[na - 1], htx.at[0], 1, 0),
                w_copy(1, wsend.at[0], htx.at[1], -1, 0)]

    def wy_copies(k, first, count):
        rows = pl.ds(first, count)
        return [w_copy(k, wsend.at[rows, nbk - 1], hty.at[0, rows], 0, 1),
                w_copy(k + 1, wsend.at[rows, 0], hty.at[1, rows], 0, -1)]

    inner_wy = wy_copies(2, 2, na - 4)
    edge_wy = wy_copies(4, 0, 1) + wy_copies(6, na - 1, 1)
    last_wy = wy_copies(8, 1, 1) + wy_copies(10, na - 2, 1)
    inner = (na - 4) // 2

    @pl.loop(0, inner + 2)
    def _(i):
        h = i // inner
        r = i - inner * h

        @pl.when(i == inner)
        def _():
            for c in inner_wy:
                c.start()
            for k in (0, 1, 4, 5, 6, 7):
                halo_copy(k).wait_recv()
            for k in range(HALO):
                for b in range(nbk + 2 * HALO):
                    grams[k, b] = landed[0, k, b]
                    grams[na + HALO + k, b] = landed[1, k, b]

        one = (1 - h) * (2 + 2 * r) + h * r
        two = (1 - h) * (3 + 2 * r) + h * (na - 1 - r)
        transform([(a, b) for a in (one, two) for b in range(nbk)])
        for b in range(1, nbk - 1):
            for a in (one, two):
                wsend[a, b] = wts[a, b].astype(BF16)

        @pl.when(i == inner)
        def _():
            for c in wx_copies() + edge_wy:
                c.start()

    for c in last_wy:
        c.start()

    def blend(a, b, lower, upper):
        left = wts[a, b - 1] if b > 0 else hty[0, a].astype(F32)
        right = wts[a, b + 1] if b < nbk - 1 else hty[1, a].astype(F32)
        out[a, b] = ((4.0 * wts[a, b] + (upper + lower) + (left + right)) * 0.125).astype(BF16)

    @pl.loop(1, na - 1)
    def _(a):
        for b in range(1, nbk - 1):
            blend(a, b, wts[a - 1, b], wts[a + 1, b])

    for c in wx_copies() + inner_wy + edge_wy:
        c.wait_recv()
    for b in range(1, nbk - 1):
        blend(0, b, htx[0, b].astype(F32), wts[1, b])
        blend(na - 1, b, wts[na - 2, b], htx[1, b].astype(F32))
    for c in last_wy:
        c.wait_recv()

    def row_out(a):
        return pltpu.make_async_copy(out.at[a], out_h.at[a], o_sem.at[a])

    for b in (0, nbk - 1):
        blend(0, b, htx[0, b].astype(F32), wts[1, b])
        blend(na - 1, b, wts[na - 2, b], htx[1, b].astype(F32))
    row_out(0).start()
    row_out(na - 1).start()

    @pl.loop(1, na - 1)
    def _(a):
        for b in (0, nbk - 1):
            blend(a, b, wts[a - 1, b], wts[a + 1, b])
        row_out(a).start()

    for k in range(8):
        halo_copy(k).wait_send()
    for c in xs + ys + wx_copies() + inner_wy + edge_wy + last_wy:
        c.wait_send()
    mean_out.wait()
    for a in range(na):
        row_out(a).wait()


def apply_weights(members_h, mean_th, blended_h, out_h, members, mean_t, blended, result, sem):
    na, nbk, levels, width = members.shape
    row = lax.broadcasted_iota(jnp.int32, (width, width), 0)

    def loads(a):
        return [pltpu.make_async_copy(src.at[a], dst.at[a], sem.at[k, a])
                for k, (src, dst) in enumerate(
                    [(blended_h, blended), (mean_th, mean_t), (members_h, members)])]

    def copy_out(a):
        return pltpu.make_async_copy(result.at[a], out_h.at[a], sem.at[3, a])

    for a in range(na):
        for c in loads(a):
            c.start()

    @pl.loop(0, na)
    def _(a):
        for c in loads(a):
            c.wait()
        for b in range(nbk):
            pick = jnp.where((row == b) | (row == b + nbk) | (row == b + 2 * nbk), 1.0, 0.0)
            left = jnp.concatenate([members[a, b], mean_t[a]], axis=1)
            right = jnp.concatenate([blended[a, b], pick.astype(BF16)], axis=0)
            result[a, b] = jnp.dot(left, right, preferred_element_type=F32).astype(BF16)
        copy_out(a).start()

    @pl.loop(0, na)
    def _(a):
        copy_out(a).wait()


def shards(nx, ny, members, mean_state, obs_pert, obs_rinv, innovation, obs_count, neighbours,
           loc_weight):
    na, nbk, slots, width = obs_pert.shape
    levels = members.shape[2]
    hbm = pl.BlockSpec(memory_space=pltpu.HBM)
    dma = pltpu.SemaphoreType.DMA
    half = width // 2
    blended, mean_t = pl.pallas_call(
        functools.partial(analysis_weights, nx, ny),
        out_shape=[
            jax.ShapeDtypeStruct((na, nbk, width, width), BF16),
            jax.ShapeDtypeStruct((na, levels, width), BF16),
        ],
        in_specs=[hbm] * 7,
        out_specs=[hbm] * 2,
        scratch_shapes=[
            pltpu.VMEM((na, nbk, width, width), BF16),
            pltpu.VMEM((na, levels, width), BF16),
            pltpu.SMEM((nbk, na), jnp.int32),
            pltpu.SMEM(neighbours.shape, jnp.int32),
            pltpu.SMEM(loc_weight.shape, F32),
            pltpu.VMEM(obs_pert.shape, BF16),
            pltpu.VMEM(obs_rinv.shape, BF16),
            pltpu.VMEM(innovation.shape, BF16),
            pltpu.VMEM(mean_state.shape, F32),
            pltpu.VMEM((na + 2 * HALO, nbk + 2 * HALO, half + 16, width), BF16),
            pltpu.VMEM((2, HALO, nbk + 2 * HALO, half + 16, width), BF16),
            pltpu.VMEM((na, nbk, width, width), F32),
            pltpu.VMEM((na, nbk, width, width), BF16),
            pltpu.VMEM((2, nbk, width, width), BF16),
            pltpu.VMEM((2, na, width, width), BF16),
            pltpu.VMEM((8, slots), F32),
            pltpu.VMEM((nx - 1, 8, slots), F32),
            pltpu.VMEM((8, slots), F32),
            pltpu.VMEM((ny - 1, 8, slots), F32),
            dma((7,)), dma((na // 2,)), dma((na,)),
            dma((8,)), dma((8,)),
            dma((nx - 1,)), dma((nx - 1,)),
            dma((ny - 1,)), dma((ny - 1,)),
            dma((12,)), dma((12,)),
        ],
        compiler_params=pltpu.CompilerParams(
            collective_id=0, has_side_effects=True, vmem_limit_bytes=57 * 1024 * 1024),
    )(obs_count.T, neighbours, loc_weight, obs_pert, obs_rinv, innovation, mean_state)
    return pl.pallas_call(
        apply_weights,
        out_shape=jax.ShapeDtypeStruct(members.shape, BF16),
        in_specs=[hbm] * 3,
        out_specs=hbm,
        scratch_shapes=[
            pltpu.VMEM(members.shape, BF16),
            pltpu.VMEM((na, levels, width), BF16),
            pltpu.VMEM((na, nbk, width, width), BF16),
            pltpu.VMEM(members.shape, BF16),
            dma((4, na)),
        ],
        compiler_params=pltpu.CompilerParams(vmem_limit_bytes=57 * 1024 * 1024),
    )(members, mean_t, blended)


def solution(mesh):
    nx, ny = mesh.shape["tx"], mesh.shape["ty"]
    return jax.shard_map(
        functools.partial(shards, nx, ny),
        mesh=mesh,
        in_specs=(
            P("tx", "ty", None, None),
            P("tx", "ty", None),
            P("tx", "ty", None, None),
            P("tx", "ty", None),
            P("tx", "ty", None),
            P("tx", "ty"),
            P("tx", "ty", None),
            P("tx", "ty", None),
        ),
        out_specs=P("tx", "ty", None, None),
        check_vma=False,
    )
```

time: 62.1 us -> 44.4 us (0.71)
  Pallas kernels: 53.7 us -> 44.2 us
  local copies, waits for them, and re-layouts: 7.83 us -> 0 us
    pallas_call x2, Pallas kernels: 53.7 us -> 44.2 us  [the longest x1 38.5 us: shards(): pl.pallas_call(functools.partial(analysis_weights, nx, ny), out_shape=[ja...]
    unnamed x15 -> x0, local copies, waits for them, and re-layouts: 7.83 us -> none
where the time goes in v2:
time: 44.4 us; the launch traced here: 44.2 us
  Pallas kernels  44.2 us (100%)
    pallas_call x1, Pallas kernels, shards(): pl.pallas_call(functools.partial(analysis_weights, nx, ny), out_shape=[ja...  38.5 us
    pallas_call x1, Pallas kernels, shards(): pl.pallas_call(apply_weights, out_shape=jax.ShapeDtypeStruct(members.shap...  5.69 us

profile of v2, /device:TPU:0, one launch (start us, length us, event | category | flops | bytes accessed | tf_op | source)
XLA Modules:
  0.0 44.2 jit_solution(1644754287886813034)
XLA Ops:
  0.0 38.5 %shard_map.82 = (bf16[8,4,128,128]{3,2,1,0:T(8,128)(2,1)}, bf16[8,512,128]{2,1,0:T(8,128)(2,1)}) custom-call(s32[4,8]{1,0:T(4,128)} %bitcast.1, s32[8,4,12]{2,1,0:T(4,128)} %nb_h.1, f32[8,4,12]{2,1,0:T(4,128)} %lw_h.1, bf16[8,4,128,128]{3,2,1,0:T(8,128)(2,1)} %pert_h.1, bf16[8,4,128]{2,1,0:T(4,128)(2,1)} %rinv_h.1, bf16[8,4,128]{2,1,0:T(4,128)(2,1)} %innov_h.1, ...), custom_call_target="tpu_custom_call" | custom-call | tf_op jit(solution)/shard_map/pallas_call | solution.py:393
  38.5 5.7 %shard_map.83 = bf16[8,4,512,128]{3,2,1,0:T(8,128)(2,1)} custom-call(bf16[8,4,512,128]{3,2,1,0:T(8,128)(2,1)} %members_h.1, bf16[8,512,128]{2,1,0:T(8,128)(2,1)} %get-tuple-element.7.mean_th, bf16[8,4,128,128]{3,2,1,0:T(8,128)(2,1)} %get-tuple-element.8.blended_h), custom_call_target="tpu_custom_call" | custom-call | tf_op jit(solution)/shard_map/pallas_call | solution.py:430

commit v3 on v2

--- a/solution.py
+++ b/solution.py
@@ -15,9 +15,7 @@
 
 
 def offsets(nx, ny):
-    found = {(dx, 0) for dx in range(1, nx)} | {(0, dy) for dy in range(1, ny)}
-    found |= {(dx % nx, dy % ny) for dx in (-1, 1) for dy in (-1, 1)}
-    return sorted(found - {(0, 0)})
+    return [(dx, 0) for dx in range(1, nx)] + [(0, dy) for dy in range(1, ny)]
 
 
 def matmul(a, b):
@@ -120,24 +118,26 @@
         grams[a + HALO, b + HALO, half:, :] = extra.astype(BF16)
         return qd * d, jnp.where(live, 1.0, 0.0) + diag * (1.0 / (width - 1))
 
-    def span(step, n):
-        if step == 0:
-            return pl.ds(HALO, n), pl.ds(HALO, n)
-        if step == 1:
-            return pl.ds(n, HALO), pl.ds(0, HALO)
-        return pl.ds(HALO, HALO), pl.ds(n + HALO, HALO)
-
-    def halo_copy(k):
-        dx, dy = directions[k]
-        sa, da = span(dx, na)
-        sb, db = span(dy, nbk)
-        target = grams.at[da, db] if dx == 0 else landed.at[(1 - dx) // 2, :, db]
+    def remote(src, dst, k, dx, dy):
         return pltpu.make_async_remote_copy(
-            src_ref=grams.at[sa, sb], dst_ref=target,
-            send_sem=g_send.at[k], recv_sem=g_recv.at[k],
+            src_ref=src, dst_ref=dst, send_sem=g_send.at[k], recv_sem=g_recv.at[k],
             device_id=at(dx, dy), device_id_type=MESH)
 
-    directions = [(1, 0), (-1, 0), (0, 1), (0, -1), (1, 1), (1, -1), (-1, 1), (-1, -1)]
+    own_cols = pl.ds(HALO, nbk)
+    ends = (pl.ds(0, HALO), pl.ds(nbk + HALO, HALO))
+
+    def tx_copies(cols, k):
+        return [remote(grams.at[pl.ds(na, HALO), cols], landed.at[0, :, cols], k, 1, 0),
+                remote(grams.at[pl.ds(HALO, HALO), cols], landed.at[1, :, cols], k + 1, -1, 0)]
+
+    def ty_copies(i):
+        rows = pl.ds(HALO + pair_at(i), 2)
+        k = 6 + 2 * i
+        return [remote(grams.at[rows, pl.ds(nbk, HALO)], grams.at[rows, ends[0]], k, 0, 1),
+                remote(grams.at[rows, pl.ds(HALO, HALO)], grams.at[rows, ends[1]], k + 1, 0, -1)]
+
+    def corner_copies():
+        return tx_copies(ends[0], 2) + tx_copies(ends[1], 4)
 
     def gram_rows(i, sums):
         first, second = sums
@@ -148,11 +148,17 @@
                 one, two = gram_terms(base + k, b)
                 first, second = first + one, second + two
 
+        @pl.when(i == 0)
+        def _():
+            pl.semaphore_wait(barrier, len(partners))
+
+        for c in ty_copies(i):
+            c.start()
+
         @pl.when(i == 1)
         def _():
-            pl.semaphore_wait(barrier, len(partners))
-            for k in (0, 1):
-                halo_copy(k).start()
+            for c in tx_copies(own_cols, 0):
+                c.start()
 
         return first, second
 
@@ -166,8 +172,6 @@
         for k in range(1, nx)]
     for c in xs:
         c.start()
-    for k in range(2, 8):
-        halo_copy(k).start()
 
     loads[5].wait()
 
@@ -199,8 +203,11 @@
         c.wait_recv()
     total = jnp.sum(st_sum[...] + jnp.sum(st_y[...], axis=0), axis=1, keepdims=True)
     inflation = (width - 1) * total[1:2] / total[0:1]
-    for k in (2, 3):
-        halo_copy(k).wait_recv()
+    for i in range(na // 2):
+        for c in ty_copies(i):
+            c.wait_recv()
+    for c in corner_copies():
+        c.start()
 
     def listed_sum(a, b):
         acc = None
@@ -287,8 +294,8 @@
         def _():
             for c in inner_wy:
                 c.start()
-            for k in (0, 1, 4, 5, 6, 7):
-                halo_copy(k).wait_recv()
+            for c in tx_copies(own_cols, 0) + corner_copies():
+                c.wait_recv()
             for k in range(HALO):
                 for b in range(nbk + 2 * HALO):
                     grams[k, b] = landed[0, k, b]
@@ -319,22 +326,11 @@
         for b in range(1, nbk - 1):
             blend(a, b, wts[a - 1, b], wts[a + 1, b])
 
-    for c in wx_copies() + inner_wy + edge_wy:
-        c.wait_recv()
-    for b in range(1, nbk - 1):
-        blend(0, b, htx[0, b].astype(F32), wts[1, b])
-        blend(na - 1, b, wts[na - 2, b], htx[1, b].astype(F32))
-    for c in last_wy:
-        c.wait_recv()
-
     def row_out(a):
         return pltpu.make_async_copy(out.at[a], out_h.at[a], o_sem.at[a])
 
-    for b in (0, nbk - 1):
-        blend(0, b, htx[0, b].astype(F32), wts[1, b])
-        blend(na - 1, b, wts[na - 2, b], htx[1, b].astype(F32))
-    row_out(0).start()
-    row_out(na - 1).start()
+    for c in inner_wy + last_wy:
+        c.wait_recv()
 
     @pl.loop(1, na - 1)
     def _(a):
@@ -342,9 +338,17 @@
             blend(a, b, wts[a - 1, b], wts[a + 1, b])
         row_out(a).start()
 
-    for k in range(8):
-        halo_copy(k).wait_send()
-    for c in xs + ys + wx_copies() + inner_wy + edge_wy + last_wy:
+    for c in edge_wy + wx_copies():
+        c.wait_recv()
+    for b in range(nbk):
+        blend(0, b, htx[0, b].astype(F32), wts[1, b])
+        blend(na - 1, b, wts[na - 2, b], htx[1, b].astype(F32))
+    row_out(0).start()
+    row_out(na - 1).start()
+    for i in range(na // 2):
+        for c in ty_copies(i):
+            c.wait_send()
+    for c in tx_copies(own_cols, 0) + corner_copies() + xs + ys + wx_copies() + inner_wy + edge_wy + last_wy:
         c.wait_send()
     mean_out.wait()
     for a in range(na):
@@ -419,7 +423,7 @@
             pltpu.VMEM((8, slots), F32),
             pltpu.VMEM((ny - 1, 8, slots), F32),
             dma((7,)), dma((na // 2,)), dma((na,)),
-            dma((8,)), dma((8,)),
+            dma((6 + na,)), dma((6 + na,)),
             dma((nx - 1,)), dma((nx - 1,)),
             dma((ny - 1,)), dma((ny - 1,)),
             dma((12,)), dma((12,)),

time: 44.4 us -> 45.4 us (1.023)
  Pallas kernels: 44.2 us -> 45.2 us
    pallas_call x1, Pallas kernels: 38.5 us -> 39.6 us  [shards(): pl.pallas_call(functools.partial(analysis_weights, nx, ny), out_shape=[ja...]
where the time goes in v3:
time: 45.4 us; the launch traced here: 45.3 us
  Pallas kernels  45.2 us (100%)
    pallas_call x1, Pallas kernels, shards(): pl.pallas_call(functools.partial(analysis_weights, nx, ny), out_shape=[ja...  39.6 us
    pallas_call x1, Pallas kernels, shards(): pl.pallas_call(apply_weights, out_shape=jax.ShapeDtypeStruct(members.shap...  5.67 us

profile of v3, /device:TPU:0, one launch (start us, length us, event | category | flops | bytes accessed | tf_op | source)
XLA Modules:
  0.0 45.3 jit_solution(8194028851332774034)
XLA Ops:
  0.0 39.6 %shard_map.82 = (bf16[8,4,128,128]{3,2,1,0:T(8,128)(2,1)}, bf16[8,512,128]{2,1,0:T(8,128)(2,1)}) custom-call(s32[4,8]{1,0:T(4,128)} %bitcast.1, s32[8,4,12]{2,1,0:T(4,128)} %nb_h.1, f32[8,4,12]{2,1,0:T(4,128)} %lw_h.1, bf16[8,4,128,128]{3,2,1,0:T(8,128)(2,1)} %pert_h.1, bf16[8,4,128]{2,1,0:T(4,128)(2,1)} %rinv_h.1, bf16[8,4,128]{2,1,0:T(4,128)(2,1)} %innov_h.1, ...), custom_call_target="tpu_custom_call" | custom-call | tf_op jit(solution)/shard_map/pallas_call | solution.py:397
  39.6 5.7 %shard_map.83 = bf16[8,4,512,128]{3,2,1,0:T(8,128)(2,1)} custom-call(bf16[8,4,512,128]{3,2,1,0:T(8,128)(2,1)} %members_h.1, bf16[8,512,128]{2,1,0:T(8,128)(2,1)} %get-tuple-element.7.mean_th, bf16[8,4,128,128]{3,2,1,0:T(8,128)(2,1)} %get-tuple-element.8.blended_h), custom_call_target="tpu_custom_call" | custom-call | tf_op jit(solution)/shard_map/pallas_call | solution.py:434

commit v4 on v3

--- a/solution.py
+++ b/solution.py
@@ -15,7 +15,9 @@
 
 
 def offsets(nx, ny):
-    return [(dx, 0) for dx in range(1, nx)] + [(0, dy) for dy in range(1, ny)]
+    found = {(dx, 0) for dx in range(1, nx)} | {(0, dy) for dy in range(1, ny)}
+    found |= {(dx % nx, dy % ny) for dx in (-1, 1) for dy in (-1, 1)}
+    return sorted(found - {(0, 0)})
 
 
 def matmul(a, b):
@@ -33,10 +35,12 @@
     return s * t, matmul(a, b) + (s * b + t * a)
 
 
-def two_sweeps(y):
+def two_sweeps(y, beside):
     sq = [square(v) for v in y]
+    beside()
     inner = [q[1] - 9.0 * v[1] for q, v in zip(sq, y)]
     cross = [matmul(q[1], i) for q, i in zip(sq, inner)]
+    beside()
     out = []
     for c, q, v in zip(cross, sq, y):
         mid = q[0] - 9.0 * v[0] + 27.0
@@ -52,7 +56,7 @@
 def analysis_weights(nx, ny, cnt_h, nb_h, lw_h, pert_h, rinv_h, innov_h, mean_h,
                      out_h, mean_th,
                      out, mean_t, cnt, nb, lw, pert, rinv, innov, mean,
-                     grams, landed, wts, wsend, htx, hty, st_own, st_x, st_sum, st_y,
+                     grams, landed, ready, ready_v, wts, wsend, htx, hty, st_own, st_x, st_sum, st_y,
                      i_sem, p_sem, o_sem, g_send, g_recv, x_send, x_recv, y_send, y_recv,
                      w_send, w_recv):
     na, nbk, slots, width = pert.shape
@@ -96,27 +100,34 @@
     sub = lax.broadcasted_iota(jnp.int32, (16, slots), 0)
     subw = lax.broadcasted_iota(jnp.int32, (16, width), 0)
 
-    def gram_terms(a, b):
-        p = pert[a, b]
-        live = lane < cnt[b, a]
-        q = jnp.where(live, rinv[a, b:b + 1, :].astype(F32), 0.0)
-        d = innov[a, b:b + 1, :].astype(F32)
-        qd = q * d
-        hi = qd.astype(BF16).astype(F32)
-        scaled = (jnp.transpose(p.astype(F32)) * q).astype(BF16)
-        tail = jnp.where(sub == 0, hi, jnp.where(sub == 1, qd - hi, 0.0))
-        g = jnp.dot(scaled, p, preferred_element_type=F32)
-        v = jnp.dot(tail.astype(BF16), p, preferred_element_type=F32)
-        diag = jnp.sum(jnp.where(eye, g, 0.0), axis=0, keepdims=True)
-        lower = pltpu.roll(g[half:], half, 1)
-        packed = jnp.where(hrow <= hlane, g[:half], lower)
-        vec = v[0:1] + v[1:2]
-        vhi = vec.astype(BF16).astype(F32)
-        extra = jnp.where(subw == 0, diag,
-                          jnp.where(subw == 1, vhi, jnp.where(subw == 2, vec - vhi, 0.0)))
-        grams[a + HALO, b + HALO, :half, :] = packed.astype(BF16)
-        grams[a + HALO, b + HALO, half:, :] = extra.astype(BF16)
-        return qd * d, jnp.where(live, 1.0, 0.0) + diag * (1.0 / (width - 1))
+    def gram_terms(blocks):
+        ps = [pert[a, b] for a, b in blocks]
+        lives = [lane < cnt[b, a] for a, b in blocks]
+        qs = [jnp.where(live, rinv[a, b:b + 1, :].astype(F32), 0.0)
+              for live, (a, b) in zip(lives, blocks)]
+        ds = [innov[a, b:b + 1, :].astype(F32) for a, b in blocks]
+        flipped = [jnp.transpose(p) for p in ps]
+        scaled = [(f.astype(F32) * q).astype(BF16) for f, q in zip(flipped, qs)]
+        qds = [q * d for q, d in zip(qs, ds)]
+        his = [qd.astype(BF16).astype(F32) for qd in qds]
+        tails = [jnp.where(sub == 0, hi, jnp.where(sub == 1, qd - hi, 0.0)).astype(BF16)
+                 for hi, qd in zip(his, qds)]
+        gs = [jnp.dot(x, p, preferred_element_type=F32) for x, p in zip(scaled, ps)]
+        vs = [jnp.dot(x, p, preferred_element_type=F32) for x, p in zip(tails, ps)]
+        diags = [jnp.sum(jnp.where(eye, g, 0.0), axis=0, keepdims=True) for g in gs]
+        lowers = [pltpu.roll(g[half:], half, 1) for g in gs]
+        packed = [jnp.where(hrow <= hlane, g[:half], lower) for g, lower in zip(gs, lowers)]
+        first = second = 0.0
+        for (a, b), pk, v, diag, qd, d, live in zip(blocks, packed, vs, diags, qds, ds, lives):
+            vec = v[0:1] + v[1:2]
+            vhi = vec.astype(BF16).astype(F32)
+            extra = jnp.where(subw == 0, diag,
+                              jnp.where(subw == 1, vhi, jnp.where(subw == 2, vec - vhi, 0.0)))
+            grams[a + HALO, b + HALO, :half, :] = pk.astype(BF16)
+            grams[a + HALO, b + HALO, half:, :] = extra.astype(BF16)
+            first = first + qd * d
+            second = second + (jnp.where(live, 1.0, 0.0) + diag * (1.0 / (width - 1)))
+        return first, second
 
     def remote(src, dst, k, dx, dy):
         return pltpu.make_async_remote_copy(
@@ -126,9 +137,10 @@
     own_cols = pl.ds(HALO, nbk)
     ends = (pl.ds(0, HALO), pl.ds(nbk + HALO, HALO))
 
-    def tx_copies(cols, k):
-        return [remote(grams.at[pl.ds(na, HALO), cols], landed.at[0, :, cols], k, 1, 0),
-                remote(grams.at[pl.ds(HALO, HALO), cols], landed.at[1, :, cols], k + 1, -1, 0)]
+    def tx_copies(src_cols, dst_cols, k, dy):
+        return [
+            remote(grams.at[pl.ds(na, HALO), src_cols], landed.at[0, :, dst_cols], k, 1, dy),
+            remote(grams.at[pl.ds(HALO, HALO), src_cols], landed.at[1, :, dst_cols], k + 1, -1, dy)]
 
     def ty_copies(i):
         rows = pl.ds(HALO + pair_at(i), 2)
@@ -137,30 +149,27 @@
                 remote(grams.at[rows, pl.ds(HALO, HALO)], grams.at[rows, ends[1]], k + 1, 0, -1)]
 
     def corner_copies():
-        return tx_copies(ends[0], 2) + tx_copies(ends[1], 4)
+        return (tx_copies(pl.ds(nbk, HALO), ends[0], 2, 1)
+                + tx_copies(pl.ds(HALO, HALO), ends[1], 4, -1))
 
     def gram_rows(i, sums):
         first, second = sums
         pert_load(i).wait()
         base = pair_at(i)
-        for k in range(2):
-            for b in range(nbk):
-                one, two = gram_terms(base + k, b)
-                first, second = first + one, second + two
-
-        @pl.when(i == 0)
+        one, two = gram_terms([(base + k, b) for k in range(2) for b in range(nbk)])
+
+        @pl.when(i == 1)
         def _():
             pl.semaphore_wait(barrier, len(partners))
-
-        for c in ty_copies(i):
-            c.start()
-
-        @pl.when(i == 1)
+            for c in ty_copies(0) + tx_copies(own_cols, own_cols, 0, 0):
+                c.start()
+
+        @pl.when(i >= 1)
         def _():
-            for c in tx_copies(own_cols, 0):
+            for c in ty_copies(i):
                 c.start()
 
-        return first, second
+        return first + one, second + two
 
     zero = jnp.zeros((1, slots), F32)
     sums = lax.fori_loop(0, na // 2, gram_rows, (zero, zero))
@@ -170,7 +179,7 @@
         src_ref=st_own, dst_ref=st_x.at[k - 1], send_sem=x_send.at[k - 1],
         recv_sem=x_recv.at[k - 1], device_id=at(k, 0), device_id_type=MESH)
         for k in range(1, nx)]
-    for c in xs:
+    for c in xs + corner_copies():
         c.start()
 
     loads[5].wait()
@@ -199,15 +208,9 @@
         c.start()
     loads[3].wait()
     loads[4].wait()
-    for c in ys:
-        c.wait_recv()
-    total = jnp.sum(st_sum[...] + jnp.sum(st_y[...], axis=0), axis=1, keepdims=True)
-    inflation = (width - 1) * total[1:2] / total[0:1]
     for i in range(na // 2):
         for c in ty_copies(i):
             c.wait_recv()
-    for c in corner_copies():
-        c.start()
 
     def listed_sum(a, b):
         acc = None
@@ -234,22 +237,39 @@
     def total_of(m):
         return jnp.sum(jnp.sum(m, axis=0, keepdims=True), axis=1, keepdims=True)
 
-    def transform(groups):
-        pairs = [unpack(listed_sum(a, b)) for a, b in groups]
-        vecs = [v for _, v in pairs]
-        ms = [jnp.where(eye, m + inflation, m) for m, _ in pairs]
+    def prepare(k, slot, group):
+        m, vec = unpack(listed_sum(*group))
+        ready[slot, k] = m
+        ready_v[slot, k] = jnp.broadcast_to(vec, (8, width))
+
+    def transform(groups, slot, later):
+        todo = list(enumerate(later))
+
+        def beside():
+            if todo:
+                prepare(todo[0][0], 1 - slot, todo.pop(0)[1])
+
+        ms = [ready[slot, k] for k in range(len(groups))]
+        vecs = [ready_v[slot, k][0:1] for k in range(len(groups))]
+        ms = [jnp.where(eye, m + inflation, m) for m in ms]
         inv = [lax.rsqrt(total_of(m * m)) for m in ms]
         mid = [total_of(jnp.where(eye, m, 0.0)) * (1.0 / width) for m in ms]
         y = [(c * i, jnp.where(eye, m - c, m) * i) for m, i, c in zip(ms, inv, mid)]
-        z2 = two_sweeps(y)
+        z2 = two_sweeps(y, beside)
         v2 = [square(z) for z in z2]
+        beside()
         t2 = [scaled_by(product(p, v), 1.0 / 256) for p, v in zip(y, v2)]
-        w = two_sweeps(t2)
+        beside()
+        w = two_sweeps(t2, beside)
         z4 = [product(z, u) for z, u in zip(z2, w)]
         v4 = [square(u) for u in w]
+        beside()
         t4 = [product(t, v) for t, v in zip(t2, v4)]
+        beside()
         z5 = [(z[0] * (768.0 - t[0]), (768.0 - t[0]) * z[1] - z[0] * t[1] - matmul(z[1], t[1]))
               for z, t in zip(z4, t4)]
+        while todo:
+            beside()
         back = 1.0 / (256 * 512)
         z5 = [scaled_by(z, back) for z in z5]
         rb = [z[1].astype(BF16) for z in z5]
@@ -263,8 +283,7 @@
             scale = math.sqrt(width - 1) * jnp.sqrt(i)
             weight = scale * jnp.where(eye, r + z, r) + shift
             wts[a, b] = weight
-            if b in (0, nbk - 1):
-                wsend[a, b] = weight.astype(BF16)
+            wsend[a, b] = weight.astype(BF16)
 
     def w_copy(k, src, dst, dx, dy):
         return pltpu.make_async_remote_copy(
@@ -285,28 +304,37 @@
     last_wy = wy_copies(8, 1, 1) + wy_copies(10, na - 2, 1)
     inner = (na - 4) // 2
 
+    def batch(i):
+        h = i // inner
+        r = i - inner * h
+        one = (1 - h) * (2 + 2 * r) + h * r
+        two = (1 - h) * (3 + 2 * r) + h * (na - 1 - r)
+        return [(a, b) for a in (one, two) for b in range(nbk)]
+
+    for k, group in enumerate(batch(0)):
+        prepare(k, 0, group)
+    for c in ys:
+        c.wait_recv()
+    total = jnp.sum(st_sum[...] + jnp.sum(st_y[...], axis=0), axis=1, keepdims=True)
+    inflation = (width - 1) * total[1:2] / total[0:1]
+
     @pl.loop(0, inner + 2)
     def _(i):
-        h = i // inner
-        r = i - inner * h
-
-        @pl.when(i == inner)
+        @pl.when(i == inner - 1)
         def _():
-            for c in inner_wy:
-                c.start()
-            for c in tx_copies(own_cols, 0) + corner_copies():
+            for c in tx_copies(own_cols, own_cols, 0, 0) + corner_copies():
                 c.wait_recv()
             for k in range(HALO):
                 for b in range(nbk + 2 * HALO):
                     grams[k, b] = landed[0, k, b]
                     grams[na + HALO + k, b] = landed[1, k, b]
 
-        one = (1 - h) * (2 + 2 * r) + h * r
-        two = (1 - h) * (3 + 2 * r) + h * (na - 1 - r)
-        transform([(a, b) for a in (one, two) for b in range(nbk)])
-        for b in range(1, nbk - 1):
-            for a in (one, two):
-                wsend[a, b] = wts[a, b].astype(BF16)
+        @pl.when(i == inner)
+        def _():
+            for c in inner_wy:
+                c.start()
+
+        transform(batch(i), i % 2, batch(i + 1 - (i + 1) // (inner + 2)))
 
         @pl.when(i == inner)
         def _():
@@ -348,7 +376,7 @@
     for i in range(na // 2):
         for c in ty_copies(i):
             c.wait_send()
-    for c in tx_copies(own_cols, 0) + corner_copies() + xs + ys + wx_copies() + inner_wy + edge_wy + last_wy:
+    for c in tx_copies(own_cols, own_cols, 0, 0) + corner_copies() + xs + ys + wx_copies() + inner_wy + edge_wy + last_wy:
         c.wait_send()
     mean_out.wait()
     for a in range(na):
@@ -414,6 +442,8 @@
             pltpu.VMEM(mean_state.shape, F32),
             pltpu.VMEM((na + 2 * HALO, nbk + 2 * HALO, half + 16, width), BF16),
             pltpu.VMEM((2, HALO, nbk + 2 * HALO, half + 16, width), BF16),
+            pltpu.VMEM((2, 2 * nbk, width, width), F32),
+            pltpu.VMEM((2, 2 * nbk, 8, width), F32),
             pltpu.VMEM((na, nbk, width, width), F32),
             pltpu.VMEM((na, nbk, width, width), BF16),
             pltpu.VMEM((2, nbk, width, width), BF16),

time: 45.4 us -> 45.5 us (level)
  no operation moved by 1% of the time
where the time goes in v4:
time: 45.5 us; the launch traced here: 45.3 us
  Pallas kernels  45.3 us (100%)
    pallas_call x1, Pallas kernels, shards(): pl.pallas_call(functools.partial(analysis_weights, nx, ny), out_shape=[ja...  39.6 us
    pallas_call x1, Pallas kernels, shards(): pl.pallas_call(apply_weights, out_shape=jax.ShapeDtypeStruct(members.shap...  5.67 us

profile of v4, /device:TPU:0, one launch (start us, length us, event | category | flops | bytes accessed | tf_op | source)
XLA Modules:
  0.0 45.3 jit_solution(13565778556546384672)
XLA Ops:
  0.0 39.6 %shard_map.82 = (bf16[8,4,128,128]{3,2,1,0:T(8,128)(2,1)}, bf16[8,512,128]{2,1,0:T(8,128)(2,1)}) custom-call(s32[4,8]{1,0:T(4,128)} %bitcast.1, s32[8,4,12]{2,1,0:T(4,128)} %nb_h.1, f32[8,4,12]{2,1,0:T(4,128)} %lw_h.1, bf16[8,4,128,128]{3,2,1,0:T(8,128)(2,1)} %pert_h.1, bf16[8,4,128]{2,1,0:T(4,128)(2,1)} %rinv_h.1, bf16[8,4,128]{2,1,0:T(4,128)(2,1)} %innov_h.1, ...), custom_call_target="tpu_custom_call" | custom-call | tf_op jit(solution)/shard_map/pallas_call | solution.py:425
  39.6 5.7 %shard_map.83 = bf16[8,4,512,128]{3,2,1,0:T(8,128)(2,1)} custom-call(bf16[8,4,512,128]{3,2,1,0:T(8,128)(2,1)} %members_h.1, bf16[8,512,128]{2,1,0:T(8,128)(2,1)} %get-tuple-element.7.mean_th, bf16[8,4,128,128]{3,2,1,0:T(8,128)(2,1)} %get-tuple-element.8.blended_h), custom_call_target="tpu_custom_call" | custom-call | tf_op jit(solution)/shard_map/pallas_call | solution.py:464

commit v5 on v4

--- a/solution.py
+++ b/solution.py
@@ -15,9 +15,7 @@
 
 
 def offsets(nx, ny):
-    found = {(dx, 0) for dx in range(1, nx)} | {(0, dy) for dy in range(1, ny)}
-    found |= {(dx % nx, dy % ny) for dx in (-1, 1) for dy in (-1, 1)}
-    return sorted(found - {(0, 0)})
+    return [(dx, 0) for dx in range(1, nx)] + [(0, dy) for dy in range(1, ny)]
 
 
 def matmul(a, b):
@@ -137,20 +135,20 @@
     own_cols = pl.ds(HALO, nbk)
     ends = (pl.ds(0, HALO), pl.ds(nbk + HALO, HALO))
 
-    def tx_copies(src_cols, dst_cols, k, dy):
+    def tx_copies():
         return [
-            remote(grams.at[pl.ds(na, HALO), src_cols], landed.at[0, :, dst_cols], k, 1, dy),
-            remote(grams.at[pl.ds(HALO, HALO), src_cols], landed.at[1, :, dst_cols], k + 1, -1, dy)]
+            remote(grams.at[pl.ds(na, HALO), own_cols], landed.at[0, :, own_cols], 0, 1, 0),
+            remote(grams.at[pl.ds(HALO, HALO), own_cols], landed.at[1, :, own_cols], 1, -1, 0)]
 
     def ty_copies(i):
         rows = pl.ds(HALO + pair_at(i), 2)
-        k = 6 + 2 * i
+        k = 4 + 2 * i
         return [remote(grams.at[rows, pl.ds(nbk, HALO)], grams.at[rows, ends[0]], k, 0, 1),
                 remote(grams.at[rows, pl.ds(HALO, HALO)], grams.at[rows, ends[1]], k + 1, 0, -1)]
 
     def corner_copies():
-        return (tx_copies(pl.ds(nbk, HALO), ends[0], 2, 1)
-                + tx_copies(pl.ds(HALO, HALO), ends[1], 4, -1))
+        return [remote(landed.at[:, :, pl.ds(nbk, HALO)], landed.at[:, :, ends[0]], 2, 0, 1),
+                remote(landed.at[:, :, pl.ds(HALO, HALO)], landed.at[:, :, ends[1]], 3, 0, -1)]
 
     def gram_rows(i, sums):
         first, second = sums
@@ -161,7 +159,7 @@
         @pl.when(i == 1)
         def _():
             pl.semaphore_wait(barrier, len(partners))
-            for c in ty_copies(0) + tx_copies(own_cols, own_cols, 0, 0):
+            for c in ty_copies(0) + tx_copies():
                 c.start()
 
         @pl.when(i >= 1)
@@ -179,7 +177,7 @@
         src_ref=st_own, dst_ref=st_x.at[k - 1], send_sem=x_send.at[k - 1],
         recv_sem=x_recv.at[k - 1], device_id=at(k, 0), device_id_type=MESH)
         for k in range(1, nx)]
-    for c in xs + corner_copies():
+    for c in xs:
         c.start()
 
     loads[5].wait()
@@ -211,6 +209,10 @@
     for i in range(na // 2):
         for c in ty_copies(i):
             c.wait_recv()
+    for c in tx_copies():
+        c.wait_recv()
+    for c in corner_copies():
+        c.start()
 
     def listed_sum(a, b):
         acc = None
@@ -322,7 +324,7 @@
     def _(i):
         @pl.when(i == inner - 1)
         def _():
-            for c in tx_copies(own_cols, own_cols, 0, 0) + corner_copies():
+            for c in corner_copies():
                 c.wait_recv()
             for k in range(HALO):
                 for b in range(nbk + 2 * HALO):
@@ -376,7 +378,7 @@
     for i in range(na // 2):
         for c in ty_copies(i):
             c.wait_send()
-    for c in tx_copies(own_cols, own_cols, 0, 0) + corner_copies() + xs + ys + wx_copies() + inner_wy + edge_wy + last_wy:
+    for c in tx_copies() + corner_copies() + xs + ys + wx_copies() + inner_wy + edge_wy + last_wy:
         c.wait_send()
     mean_out.wait()
     for a in range(na):
@@ -453,7 +455,7 @@
             pltpu.VMEM((8, slots), F32),
             pltpu.VMEM((ny - 1, 8, slots), F32),
             dma((7,)), dma((na // 2,)), dma((na,)),
-            dma((6 + na,)), dma((6 + na,)),
+            dma((4 + na,)), dma((4 + na,)),
             dma((nx - 1,)), dma((nx - 1,)),
             dma((ny - 1,)), dma((ny - 1,)),
             dma((12,)), dma((12,)),

time: 45.5 us -> 42.3 us (0.930)
  Pallas kernels: 45.3 us -> 42.1 us
    pallas_call x1, Pallas kernels: 39.6 us -> 36.4 us  [shards(): pl.pallas_call(functools.partial(analysis_weights, nx, ny), out_shape=[ja...]
where the time goes in v5:
time: 42.3 us; the launch traced here: 42.1 us
  Pallas kernels  42.1 us (100%)
    pallas_call x1, Pallas kernels, shards(): pl.pallas_call(functools.partial(analysis_weights, nx, ny), out_shape=[ja...  36.4 us
    pallas_call x1, Pallas kernels, shards(): pl.pallas_call(apply_weights, out_shape=jax.ShapeDtypeStruct(members.shap...  5.67 us

profile of v5, /device:TPU:0, one launch (start us, length us, event | category | flops | bytes accessed | tf_op | source)
XLA Modules:
  0.0 42.1 jit_solution(13650939608937084490)
XLA Ops:
  0.0 36.4 %shard_map.82 = (bf16[8,4,128,128]{3,2,1,0:T(8,128)(2,1)}, bf16[8,512,128]{2,1,0:T(8,128)(2,1)}) custom-call(s32[4,8]{1,0:T(4,128)} %bitcast.1, s32[8,4,12]{2,1,0:T(4,128)} %nb_h.1, f32[8,4,12]{2,1,0:T(4,128)} %lw_h.1, bf16[8,4,128,128]{3,2,1,0:T(8,128)(2,1)} %pert_h.1, bf16[8,4,128]{2,1,0:T(4,128)(2,1)} %rinv_h.1, bf16[8,4,128]{2,1,0:T(4,128)(2,1)} %innov_h.1, ...), custom_call_target="tpu_custom_call" | custom-call | tf_op jit(solution)/shard_map/pallas_call | solution.py:427
  36.4 5.7 %shard_map.83 = bf16[8,4,512,128]{3,2,1,0:T(8,128)(2,1)} custom-call(bf16[8,4,512,128]{3,2,1,0:T(8,128)(2,1)} %members_h.1, bf16[8,512,128]{2,1,0:T(8,128)(2,1)} %get-tuple-element.7.mean_th, bf16[8,4,128,128]{3,2,1,0:T(8,128)(2,1)} %get-tuple-element.8.blended_h), custom_call_target="tpu_custom_call" | custom-call | tf_op jit(solution)/shard_map/pallas_call | solution.py:466

commit v6 on v5

--- a/solution.py
+++ b/solution.py
@@ -156,16 +156,17 @@
         base = pair_at(i)
         one, two = gram_terms([(base + k, b) for k in range(2) for b in range(nbk)])
 
+        @pl.when(i == 0)
+        def _():
+            pl.semaphore_wait(barrier, len(partners))
+            tx_copies()[1].start()
+
         @pl.when(i == 1)
         def _():
-            pl.semaphore_wait(barrier, len(partners))
-            for c in ty_copies(0) + tx_copies():
-                c.start()
-
-        @pl.when(i >= 1)
-        def _():
-            for c in ty_copies(i):
-                c.start()
+            tx_copies()[0].start()
+
+        for c in ty_copies(i):
+            c.start()
 
         return first + one, second + two
 
@@ -182,16 +183,13 @@
 
     loads[5].wait()
 
-    @pl.loop(0, na)
-    def _(a):
-        row = mean[a]
-        high = row.astype(BF16).astype(F32)
-        rest = row - high
-        middle = rest.astype(BF16).astype(F32)
-        fill = jnp.zeros((width - 3 * nbk, row.shape[1]), F32)
-        stack = jnp.concatenate([high, middle, rest - middle, fill], axis=0)
-        mean_t[a] = jnp.transpose(stack).astype(BF16)
-
+    row = jnp.concatenate([mean[a] for a in range(na)], axis=0)
+    high = row.astype(BF16).astype(F32)
+    rest = row - high
+    middle = rest.astype(BF16).astype(F32)
+    fill = jnp.zeros((width - 3 * na * nbk, row.shape[1]), F32)
+    stack = jnp.concatenate([high, middle, rest - middle, fill], axis=0)
+    mean_t[...] = jnp.transpose(stack).astype(BF16)
     mean_out = pltpu.make_async_copy(mean_t, mean_th, i_sem.at[6])
     mean_out.start()
 
@@ -206,13 +204,13 @@
         c.start()
     loads[3].wait()
     loads[4].wait()
-    for i in range(na // 2):
-        for c in ty_copies(i):
-            c.wait_recv()
     for c in tx_copies():
         c.wait_recv()
     for c in corner_copies():
         c.start()
+    for i in range(na // 2):
+        for c in ty_copies(i):
+            c.wait_recv()
 
     def listed_sum(a, b):
         acc = None
@@ -392,22 +390,27 @@
     def loads(a):
         return [pltpu.make_async_copy(src.at[a], dst.at[a], sem.at[k, a])
                 for k, (src, dst) in enumerate(
-                    [(blended_h, blended), (mean_th, mean_t), (members_h, members)])]
+                    [(blended_h, blended), (members_h, members)])]
 
     def copy_out(a):
         return pltpu.make_async_copy(result.at[a], out_h.at[a], sem.at[3, a])
 
+    mean_load = pltpu.make_async_copy(mean_th, mean_t, sem.at[2, 0])
+    mean_load.start()
     for a in range(na):
         for c in loads(a):
             c.start()
+    mean_load.wait()
 
     @pl.loop(0, na)
     def _(a):
         for c in loads(a):
             c.wait()
         for b in range(nbk):
-            pick = jnp.where((row == b) | (row == b + nbk) | (row == b + 2 * nbk), 1.0, 0.0)
-            left = jnp.concatenate([members[a, b], mean_t[a]], axis=1)
+            here = a * nbk + b
+            pick = jnp.where((row == here) | (row == here + na * nbk) | (row == here + 2 * na * nbk),
+                             1.0, 0.0)
+            left = jnp.concatenate([members[a, b], mean_t[...]], axis=1)
             right = jnp.concatenate([blended[a, b], pick.astype(BF16)], axis=0)
             result[a, b] = jnp.dot(left, right, preferred_element_type=F32).astype(BF16)
         copy_out(a).start()
@@ -428,13 +431,13 @@
         functools.partial(analysis_weights, nx, ny),
         out_shape=[
             jax.ShapeDtypeStruct((na, nbk, width, width), BF16),
-            jax.ShapeDtypeStruct((na, levels, width), BF16),
+            jax.ShapeDtypeStruct((levels, width), BF16),
         ],
         in_specs=[hbm] * 7,
         out_specs=[hbm] * 2,
         scratch_shapes=[
             pltpu.VMEM((na, nbk, width, width), BF16),
-            pltpu.VMEM((na, levels, width), BF16),
+            pltpu.VMEM((levels, width), BF16),
             pltpu.SMEM((nbk, na), jnp.int32),
             pltpu.SMEM(neighbours.shape, jnp.int32),
             pltpu.SMEM(loc_weight.shape, F32),
@@ -470,7 +473,7 @@
         out_specs=hbm,
         scratch_shapes=[
             pltpu.VMEM(members.shape, BF16),
-            pltpu.VMEM((na, levels, width), BF16),
+            pltpu.VMEM((levels, width), BF16),
             pltpu.VMEM((na, nbk, width, width), BF16),
             pltpu.VMEM(members.shape, BF16),
             dma((4, na)),

time: 42.3 us -> 42.5 us (level)
  no operation moved by 1% of the time
where the time goes in v6:
time: 42.5 us; the launch traced here: 42.3 us
  Pallas kernels  42.3 us (100%)
    pallas_call x1, Pallas kernels, shards(): pl.pallas_call(functools.partial(analysis_weights, nx, ny), out_shape=[ja...  36.4 us
    pallas_call x1, Pallas kernels, shards(): pl.pallas_call(apply_weights, out_shape=jax.ShapeDtypeStruct(members.shap...  5.92 us

profile of v6, /device:TPU:0, one launch (start us, length us, event | category | flops | bytes accessed | tf_op | source)
XLA Modules:
  0.0 42.3 jit_solution(8865516577029378293)
XLA Ops:
  0.0 36.4 %shard_map.82 = (bf16[8,4,128,128]{3,2,1,0:T(8,128)(2,1)}, bf16[512,128]{1,0:T(8,128)(2,1)}) custom-call(s32[4,8]{1,0:T(4,128)} %bitcast.1, s32[8,4,12]{2,1,0:T(4,128)} %nb_h.1, f32[8,4,12]{2,1,0:T(4,128)} %lw_h.1, bf16[8,4,128,128]{3,2,1,0:T(8,128)(2,1)} %pert_h.1, bf16[8,4,128]{2,1,0:T(4,128)(2,1)} %rinv_h.1, bf16[8,4,128]{2,1,0:T(4,128)(2,1)} %innov_h.1, ...), custom_call_target="tpu_custom_call" | custom-call | tf_op jit(solution)/shard_map/pallas_call | solution.py:430
  36.4 5.9 %shard_map.83 = bf16[8,4,512,128]{3,2,1,0:T(8,128)(2,1)} custom-call(bf16[8,4,512,128]{3,2,1,0:T(8,128)(2,1)} %members_h.1, bf16[512,128]{1,0:T(8,128)(2,1)} %get-tuple-element.7.mean_th, bf16[8,4,128,128]{3,2,1,0:T(8,128)(2,1)} %get-tuple-element.8.blended_h), custom_call_target="tpu_custom_call" | custom-call | tf_op jit(solution)/shard_map/pallas_call | solution.py:469

commit v7 on v5

--- a/solution.py
+++ b/solution.py
@@ -401,16 +401,23 @@
         for c in loads(a):
             c.start()
 
-    @pl.loop(0, na)
-    def _(a):
-        for c in loads(a):
-            c.wait()
-        for b in range(nbk):
-            pick = jnp.where((row == b) | (row == b + nbk) | (row == b + 2 * nbk), 1.0, 0.0)
-            left = jnp.concatenate([members[a, b], mean_t[a]], axis=1)
-            right = jnp.concatenate([blended[a, b], pick.astype(BF16)], axis=0)
-            result[a, b] = jnp.dot(left, right, preferred_element_type=F32).astype(BF16)
-        copy_out(a).start()
+    picks = [jnp.where((row == b) | (row == b + nbk) | (row == b + 2 * nbk), 1.0, 0.0).astype(BF16)
+             for b in range(nbk)]
+
+    @pl.loop(0, na // 2)
+    def _(i):
+        pair = (2 * i, 2 * i + 1)
+        for a in pair:
+            for c in loads(a):
+                c.wait()
+        groups = [(a, b) for a in pair for b in range(nbk)]
+        lefts = [jnp.concatenate([members[a, b], mean_t[a]], axis=1) for a, b in groups]
+        rights = [jnp.concatenate([blended[a, b], picks[b]], axis=0) for a, b in groups]
+        values = [jnp.dot(x, y, preferred_element_type=F32) for x, y in zip(lefts, rights)]
+        for (a, b), value in zip(groups, values):
+            result[a, b] = value.astype(BF16)
+        for a in pair:
+            copy_out(a).start()
 
     @pl.loop(0, na)
     def _(a):

time: 42.3 us -> 42.1 us (level)
  no operation moved by 1% of the time
where the time goes in v7:
time: 42.1 us; the launch traced here: 41.9 us
  Pallas kernels  41.9 us (100%)
    pallas_call x1, Pallas kernels, shards(): pl.pallas_call(functools.partial(analysis_weights, nx, ny), out_shape=[ja...  36.4 us
    pallas_call x1, Pallas kernels, shards(): pl.pallas_call(apply_weights, out_shape=jax.ShapeDtypeStruct(members.shap...  5.48 us

profile of v7, /device:TPU:0, one launch (start us, length us, event | category | flops | bytes accessed | tf_op | source)
XLA Modules:
  0.0 41.9 jit_solution(6810002779740667869)
XLA Ops:
  0.0 36.4 %shard_map.82 = (bf16[8,4,128,128]{3,2,1,0:T(8,128)(2,1)}, bf16[8,512,128]{2,1,0:T(8,128)(2,1)}) custom-call(s32[4,8]{1,0:T(4,128)} %bitcast.1, s32[8,4,12]{2,1,0:T(4,128)} %nb_h.1, f32[8,4,12]{2,1,0:T(4,128)} %lw_h.1, bf16[8,4,128,128]{3,2,1,0:T(8,128)(2,1)} %pert_h.1, bf16[8,4,128]{2,1,0:T(4,128)(2,1)} %rinv_h.1, bf16[8,4,128]{2,1,0:T(4,128)(2,1)} %innov_h.1, ...), custom_call_target="tpu_custom_call" | custom-call | tf_op jit(solution)/shard_map/pallas_call | solution.py:434
  36.4 5.5 %shard_map.83 = bf16[8,4,512,128]{3,2,1,0:T(8,128)(2,1)} custom-call(bf16[8,4,512,128]{3,2,1,0:T(8,128)(2,1)} %members_h.1, bf16[8,512,128]{2,1,0:T(8,128)(2,1)} %get-tuple-element.7.mean_th, bf16[8,4,128,128]{3,2,1,0:T(8,128)(2,1)} %get-tuple-element.8.blended_h), custom_call_target="tpu_custom_call" | custom-call | tf_op jit(solution)/shard_map/pallas_call | solution.py:473

commit v8 on v5

--- a/solution.py
+++ b/solution.py
@@ -320,7 +320,7 @@
     total = jnp.sum(st_sum[...] + jnp.sum(st_y[...], axis=0), axis=1, keepdims=True)
     inflation = (width - 1) * total[1:2] / total[0:1]
 
-    @pl.loop(0, inner + 2)
+    @pl.loop(0, inner + 1)
     def _(i):
         @pl.when(i == inner - 1)
         def _():
@@ -336,13 +336,14 @@
             for c in inner_wy:
                 c.start()
 
-        transform(batch(i), i % 2, batch(i + 1 - (i + 1) // (inner + 2)))
+        transform(batch(i), i % 2, batch(i + 1))
 
         @pl.when(i == inner)
         def _():
             for c in wx_copies() + edge_wy:
                 c.start()
 
+    transform(batch(inner + 1), (inner + 1) % 2, [])
     for c in last_wy:
         c.start()
 

time: 42.3 us -> 41.8 us (0.988)
  Pallas kernels: 42.1 us -> 41.6 us
    pallas_call x1, Pallas kernels: 36.4 us -> 35.9 us  [shards(): pl.pallas_call(functools.partial(analysis_weights, nx, ny), out_shape=[ja...]
where the time goes in v8:
time: 41.8 us; the launch traced here: 41.6 us
  Pallas kernels  41.6 us (100%)
    pallas_call x1, Pallas kernels, shards(): pl.pallas_call(functools.partial(analysis_weights, nx, ny), out_shape=[ja...  35.9 us
    pallas_call x1, Pallas kernels, shards(): pl.pallas_call(apply_weights, out_shape=jax.ShapeDtypeStruct(members.shap...  5.67 us

profile of v8, /device:TPU:0, one launch (start us, length us, event | category | flops | bytes accessed | tf_op | source)
XLA Modules:
  0.0 41.6 jit_solution(119840062092883639)
XLA Ops:
  0.0 35.9 %shard_map.82 = (bf16[8,4,128,128]{3,2,1,0:T(8,128)(2,1)}, bf16[8,512,128]{2,1,0:T(8,128)(2,1)}) custom-call(s32[4,8]{1,0:T(4,128)} %bitcast.1, s32[8,4,12]{2,1,0:T(4,128)} %nb_h.1, f32[8,4,12]{2,1,0:T(4,128)} %lw_h.1, bf16[8,4,128,128]{3,2,1,0:T(8,128)(2,1)} %pert_h.1, bf16[8,4,128]{2,1,0:T(4,128)(2,1)} %rinv_h.1, bf16[8,4,128]{2,1,0:T(4,128)(2,1)} %innov_h.1, ...), custom_call_target="tpu_custom_call" | custom-call | tf_op jit(solution)/shard_map/pallas_call | solution.py:428
  35.9 5.7 %shard_map.83 = bf16[8,4,512,128]{3,2,1,0:T(8,128)(2,1)} custom-call(bf16[8,4,512,128]{3,2,1,0:T(8,128)(2,1)} %members_h.1, bf16[8,512,128]{2,1,0:T(8,128)(2,1)} %get-tuple-element.7.mean_th, bf16[8,4,128,128]{3,2,1,0:T(8,128)(2,1)} %get-tuple-element.8.blended_h), custom_call_target="tpu_custom_call" | custom-call | tf_op jit(solution)/shard_map/pallas_call | solution.py:467
